TPU v7x, 512 devices: a whole 4x8x8 slice. The times are simulated.
512 devices in a mesh: wide: 128 (over z, y, core), narrow: 4 (over x).
Axes of the slice: x: 4, y: 8, z: 8, core: 2. Of those that a mesh axis runs over, the one named last changes fastest.
Arguments:
- rhs: float32 [2048, 32, 128], P('wide', 'narrow'), may hold values from -4 to 6
- coefficient: float32 [2048, 32, 128], P('wide', 'narrow'), may hold values from 0.125 to 8
- guess: float32 [2048, 32, 128], P('wide', 'narrow'), may hold values from -6 to 6
Outputs:
- pressure: float32 [2048, 32, 128], P('wide', 'narrow')
- residual: float32 [2048, 32, 128], P('wide', 'narrow')
All inputs are finite; a program needn't handle non-finite values.
Results may differ from a plain program's by a relative error of at most 0.0003.
Values sent between devices are 32-bit elements; how exact they have to be, the bound alone decides.
No kernel may reach another device: no remote copies, remote signals or barrier semaphores. Data moves between devices by JAX's collectives and lax.ppermute only.
A program may use at most 128 MiB of HBM per device.

v0:
```python
import jax
import jax.numpy as jnp
from jax import lax
from jax.sharding import PartitionSpec as P

ITERS = 20


def padded_2(block, sides, width):
    for axis, dim in sides:
        count = lax.axis_size(axis)
        forward = [(i, i + 1) for i in range(count - 1)]
        backward = [(target, source) for source, target in forward]
        low = lax.ppermute(
            lax.slice_in_dim(block, block.shape[dim] - width, None, axis=dim), axis, forward
        )
        high = lax.ppermute(lax.slice_in_dim(block, 0, width, axis=dim), axis, backward)
        block = jnp.concatenate([low, block, high], axis=dim)
    return block


def shifts(field):
    padded = jnp.pad(field, 1)
    return [
        padded[2:, 1:-1, 1:-1],
        padded[:-2, 1:-1, 1:-1],
        padded[1:-1, 2:, 1:-1],
        padded[1:-1, :-2, 1:-1],
        padded[1:-1, 1:-1, 2:],
        padded[1:-1, 1:-1, :-2],
    ]


def weights(conduct):
    faces = [0.5 * (conduct + other) for other in shifts(conduct)]
    total = faces[0]
    for face in faces[1:]:
        total = total + face
    return (faces, total)


def beside_all(faces, field):
    near = shifts(field)
    total = faces[0] * near[0]
    for index in range(1, 6):
        total = total + faces[index] * near[index]
    return total


def restrict(field):
    sx, sz, sy = field.shape
    return jnp.sum(field.reshape(sx // 2, 2, sz // 2, 2, sy // 2, 2), axis=(1, 3, 5)) * 0.125


def prolong(field):
    return jnp.repeat(jnp.repeat(jnp.repeat(field, 2, axis=0), 2, axis=1), 2, axis=2)


def trimmed(array):
    return array[1:-1, 1:-1]


def setup(conduct, source, scale):
    cells_x, cells_z, cells_y = conduct.shape
    extended = padded_2(jnp.stack([conduct, source]), (("wide", 1), ("narrow", 2)), 2)
    faces, diag = weights(extended[0])
    diag = jnp.where(diag > 0.0, diag, 1.0)
    glob_x = lax.axis_index("wide") * cells_x + jnp.arange(-2, cells_x + 2, dtype=jnp.int32)
    glob_z = lax.axis_index("narrow") * cells_z + jnp.arange(-2, cells_z + 2, dtype=jnp.int32)
    limit_x = cells_x * lax.axis_size("wide")
    limit_z = cells_z * lax.axis_size("narrow")
    inside = ((glob_x >= 0) & (glob_x < limit_x))[:, None, None] & (
        (glob_z >= 0) & (glob_z < limit_z)
    )[None, :, None]
    across = jnp.arange(cells_y, dtype=jnp.int32)
    colour = (glob_x[:, None, None] + glob_z[None, :, None] + across[None, None, :]) % 2
    return (faces, diag, extended[1], inside, colour, scale)


def smooth(field, level):
    faces, diag, source, inside, colour, scale = level
    inner_faces = [trimmed(face) for face in faces]
    inner_diag = trimmed(diag)
    inner_source = trimmed(source) / scale
    inner_colour = trimmed(colour)
    for sweep in range(2):
        for parity in (0, 1):
            wider = padded_2(field, (("wide", 0), ("narrow", 1)), 1)
            fresh = (inner_source + beside_all(inner_faces, wider)) / inner_diag
            field = trimmed(jnp.where(inner_colour == parity, fresh, wider))
    return field


def defect(field, level):
    faces, diag, source, inside, colour, scale = level
    inner_faces = [trimmed(face) for face in faces]
    wider = padded_2(field, (("wide", 0), ("narrow", 1)), 1)
    result = trimmed(source) - scale * (trimmed(diag) * wider - beside_all(inner_faces, wider))
    return trimmed(result)


def bottom(source, faces, diag, scale):

    def advance(step, carry):
        answer, remain, search, norm_now = carry
        image = scale * (diag * search - beside_all(faces, search))
        alpha = norm_now / jnp.sum(search * image)
        answer = answer + alpha * search
        remain = remain - alpha * image
        norm_next = jnp.sum(remain * remain)
        search = remain + norm_next / norm_now * search
        return (answer, remain, search, norm_next)

    start = (jnp.zeros_like(source), source, source, jnp.sum(source * source))
    return lax.fori_loop(0, ITERS, advance, start)[0]


def local(rhs, coefficient, guess):
    conduct = coefficient
    source = rhs
    field = guess
    levels = []
    fields = []
    for level_index in range(3):
        scale = 0.25**level_index
        if level_index > 0:
            field = jnp.zeros_like(source)
        level = setup(conduct, source, scale)
        field = smooth(field, level)
        levels.append(level)
        fields.append(field)
        source = restrict(defect(field, level))
        conduct = restrict(conduct)
    coarse = jnp.stack([conduct, source])
    partial_grid = lax.all_gather(coarse, "wide", axis=1, tiled=True)
    whole = lax.all_gather(partial_grid, "narrow", axis=2, tiled=True)
    faces, diag = weights(whole[0])
    solved = bottom(whole[1], faces, diag, 0.25**3)
    cells_x, cells_z, cells_y = conduct.shape
    correction = lax.dynamic_slice(
        solved,
        (lax.axis_index("wide") * cells_x, lax.axis_index("narrow") * cells_z, jnp.int32(0)),
        (cells_x, cells_z, cells_y),
    )
    for level_index in (2, 1, 0):
        field = fields[level_index] + prolong(correction)
        field = smooth(field, levels[level_index])
        correction = field
    return (field, defect(field, levels[0]))


def solution(mesh):
    return jax.shard_map(
        local,
        mesh=mesh,
        in_specs=(P("wide", "narrow", None), P("wide", "narrow", None), P("wide", "narrow", None)),
        out_specs=(P("wide", "narrow", None), P("wide", "narrow", None)),
        check_vma=False,
    )
```

profile of v0, /device:TPU:249, one launch (start us, length us, event | category | flops | bytes accessed | tf_op | source)
XLA Modules:
  0.0 993.5 jit_solution(11641512100340107518)
XLA Ops:
  9.0 7.0 collective-permute-start.4
  59.6 7.7 collective-permute-done.9
  79.1 6.1 divide_select_fusion.6
  87.5 6.6 collective-permute-start.12
  100.5 7.7 collective-permute-done.13
  133.9 7.7 collective-permute-done.17
  160.8 5.5 reshape.236
  189.6 5.6 reshape.237
  197.7 5.8 collective-permute-start.24
  227.9 8.0 collective-permute-start.32
  238.4 7.0 collective-permute-start.52
  262.3 8.4 collective-permute-start.36
  327.0 5.4 collective-permute-done.45
  366.1 8.0 collective-permute-start.56
  376.1 6.3 collective-permute-done.57
  394.5 6.3 collective-permute-done.61
  412.3 6.3 collective-permute-done.65
  452.7 53.1 %all_gather.6 = f32[2,256,1,16]{3,0,2,1:T(2,128)} all-gather(f32[2,2,1,16]{3,0,2,1:T(2,128)S(1)} %copy.320), channel_id=1, replica_groups=mesh['wide'=128,'narrow'=4] {'wide'}, dimensions={1}, use_global_device_ids=true | all-gather | bytes 33024 | tf_op jit(solution)/shard_map/all_gather | solution.py:135
  507.5 9.3 all_gather.7
  518.3 148.6 %while.19 = (s32[]{:T(128)}, f32[256,4,16]{0,2,1:T(8,128)}, f32[256,4,16]{0,2,1:T(8,128)S(1)}, f32[256,4,16]{0,2,1:T(8,128)S(1)}, f32[]{:T(128)}, /*index=5*/f32...) while((s32[]{:T(128)}, f32[256,4,16]{0,2,1:T(8,128)}, ...), condition=%wide.region_12.13_spmd.clone, body=%wide.region_9.12_spmd.clone.sunk | while | flops 409604 | bytes 1114327 | solution.py:115
  668.7 7.2 collective-permute-start.72
  677.8 6.3 collective-permute-done.73
  695.8 6.3 collective-permute-done.77
  716.4 6.3 collective-permute-done.81
  735.0 6.3 collective-permute-done.85
  757.4 6.7 collective-permute-done.89
  832.6 5.2 collective-permute-done.101
  859.6 7.7 collective-permute-done.105
  887.7 7.7 collective-permute-done.109
  915.7 7.7 collective-permute-done.113
  943.5 7.7 collective-permute-done.117
  971.3 7.7 collective-permute-done.121
  (717 shorter events, 689.2 us)
Async XLA Ops:
  1.4 27.7 %collective-permute-start = (f32[2,2,8,128]{3,2,1,0:T(8,128)S(1)}, f32[2,2,8,128]{3,2,1,0:T(8,128)S(1)}, u32[]{:S(2)}, u32[]{:S(2)}) collective-permute-start(f32[2,2,8,128]{3,2,1,0:T(8,128)S(1)} %get-tuple-element.421), channel_id=1, source_target_pairs={{0,4},{4,8},{8,12},{12,16},{16,20},{20,24},{24,28},{28,32},{32,36}... | collective-permute-start | bytes 49160 | tf_op jit(solution)/shard_map/ppermute | solution.py:14
  6.4 22.8 %collective-permute-start.1 = (f32[2,2,8,128]{3,2,1,0:T(8,128)S(1)}, f32[2,2,8,128]{3,2,1,0:T(8,128)S(1)}, u32[]{:S(2)}, u32[]{:S(2)}) collective-permute-start(f32[2,2,8,128]{3,2,1,0:T(8,128)S(1)} %get-tuple-element.422), channel_id=1, source_target_pairs={{4,0},{8,4},{12,8},{16,12},{20,16},{24,20},{28,24},{32,28},{36,32}... | collective-permute-start | bytes 49160 | tf_op jit(solution)/shard_map/ppermute | solution.py:17
  9.0 10.3 %collective-permute-start.4 = (f32[1,8,128]{2,1,0:T(8,128)S(1)}, f32[1,8,128]{2,1,0:T(8,128)S(1)}, u32[]{:S(2)}, u32[]{:S(2)}) collective-permute-start(f32[1,8,128]{2,1,0:T(8,128)S(1)} %get-tuple-element.428), channel_id=1, source_target_pairs={{0,4},{4,8},{8,12},{12,16},{16,20},{20,24},{24,28},{28,32},{32,36}... | collective-permute-start | bytes 12296 | tf_op jit(solution)/shard_map/ppermute | solution.py:14
  24.6 10.3 %collective-permute-start.6 = (f32[18,1,128]{0,1,2:T(1,128)S(1)}, f32[18,1,128]{0,1,2:T(1,128)S(1)}, u32[]{:S(2)}, u32[]{:S(2)}) collective-permute-start(f32[18,1,128]{0,1,2:T(1,128)S(1)} %copy.290), channel_id=1, source_target_pairs={{0,1},{1,2},{2,3},{4,5},{5,6},{6,7},{8,9},{9,10},{10,11},{12,13},{... | collective-permute-start | bytes 27656 | tf_op jit(solution)/shard_map/ppermute | solution.py:14
  49.4 10.2 %collective-permute-start.8 = (f32[1,8,128]{0,1,2:T(8,128)S(1)}, f32[1,8,128]{0,1,2:T(8,128)S(1)}, u32[]{:S(2)}, u32[]{:S(2)}) collective-permute-start(f32[1,8,128]{0,1,2:T(8,128)S(1)} %get-tuple-element.370), channel_id=1, source_target_pairs={{0,4},{4,8},{8,12},{12,16},{16,20},{20,24},{24,28},{28,32},{32,36}... | collective-permute-start | bytes 12296 | tf_op jit(solution)/shard_map/ppermute | solution.py:14
  53.5 13.8 %collective-permute-start.9 = (f32[1,8,128]{0,1,2:T(8,128)S(1)}, f32[1,8,128]{0,1,2:T(8,128)S(1)}, u32[]{:S(2)}, u32[]{:S(2)}) collective-permute-start(f32[1,8,128]{0,1,2:T(8,128)S(1)} %get-tuple-element.371), channel_id=1, source_target_pairs={{4,0},{8,4},{12,8},{16,12},{20,16},{24,20},{28,24},{32,28},{36,32}... | collective-permute-start | bytes 12296 | tf_op jit(solution)/shard_map/ppermute | solution.py:17
  72.5 132.9 %collective-permute-start.28 = (f32[1,4,64]{2,1,0:T(4,128)S(1)}, f32[1,4,64]{2,1,0:T(4,128)S(1)}, u32[]{:S(2)}, u32[]{:S(2)}) collective-permute-start(f32[1,4,64]{2,1,0:T(4,128)S(1)} %broadcast.359), channel_id=1, source_target_pairs={{0,4},{4,8},{8,12},{12,16},{16,20},{20,24},{24,28},{28,32},{32,36}... | collective-permute-start | bytes 3080 | tf_op jit(solution)/shard_map/ppermute | solution.py:14
  74.6 130.9 %collective-permute-start.29 = (f32[1,4,64]{2,1,0:T(4,128)S(1)}, f32[1,4,64]{2,1,0:T(4,128)S(1)}, u32[]{:S(2)}, u32[]{:S(2)}) collective-permute-start(f32[1,4,64]{2,1,0:T(4,128)S(1)} %broadcast.359), channel_id=1, source_target_pairs={{4,0},{8,4},{12,8},{16,12},{20,16},{24,20},{28,24},{32,28},{36,32}... | collective-permute-start | bytes 3080 | tf_op jit(solution)/shard_map/ppermute | solution.py:17
  87.5 13.0 %collective-permute-start.12 = (f32[1,8,128]{0,1,2:T(8,128)}, f32[1,8,128]{0,1,2:T(8,128)}, u32[]{:S(2)}, u32[]{:S(2)}) collective-permute-start(f32[1,8,128]{0,1,2:T(8,128)} %get-tuple-element.368), channel_id=1, source_target_pairs={{0,4},{4,8},{8,12},{12,16},{16,20},{20,24},{24,28},{28,32},{32,36}... | collective-permute-start | bytes 12296 | tf_op jit(solution)/shard_map/ppermute | solution.py:14
  94.1 14.1 %collective-permute-start.13 = (f32[1,8,128]{0,1,2:T(8,128)}, f32[1,8,128]{0,1,2:T(8,128)}, u32[]{:S(2)}, u32[]{:S(2)}) collective-permute-start(f32[1,8,128]{0,1,2:T(8,128)} %get-tuple-element.369), channel_id=1, source_target_pairs={{4,0},{8,4},{12,8},{16,12},{20,16},{24,20},{28,24},{32,28},{36,32}... | collective-permute-start | bytes 12296 | tf_op jit(solution)/shard_map/ppermute | solution.py:17
  127.8 13.8 %collective-permute-start.17 = (f32[1,8,128]{0,1,2:T(8,128)S(1)}, f32[1,8,128]{0,1,2:T(8,128)S(1)}, u32[]{:S(2)}, u32[]{:S(2)}) collective-permute-start(f32[1,8,128]{0,1,2:T(8,128)S(1)} %get-tuple-element.367), channel_id=1, source_target_pairs={{4,0},{8,4},{12,8},{16,12},{20,16},{24,20},{28,24},{32,28},{36,32}... | collective-permute-start | bytes 12296 | tf_op jit(solution)/shard_map/ppermute | solution.py:17
  155.6 14.7 %collective-permute-start.20 = (f32[1,8,128]{0,1,2:T(8,128)}, f32[1,8,128]{0,1,2:T(8,128)}, u32[]{:S(2)}, u32[]{:S(2)}) collective-permute-start(f32[1,8,128]{0,1,2:T(8,128)} %get-tuple-element.364), channel_id=1, source_target_pairs={{0,4},{4,8},{8,12},{12,16},{16,20},{20,24},{24,28},{28,32},{32,36}... | collective-permute-start | bytes 12296 | tf_op jit(solution)/shard_map/ppermute | solution.py:14
  158.8 14.1 %collective-permute-start.21 = (f32[1,8,128]{0,1,2:T(8,128)}, f32[1,8,128]{0,1,2:T(8,128)}, u32[]{:S(2)}, u32[]{:S(2)}) collective-permute-start(f32[1,8,128]{0,1,2:T(8,128)} %get-tuple-element.365), channel_id=1, source_target_pairs={{4,0},{8,4},{12,8},{16,12},{20,16},{24,20},{28,24},{32,28},{36,32}... | collective-permute-start | bytes 12296 | tf_op jit(solution)/shard_map/ppermute | solution.py:17
  197.7 10.7 %collective-permute-start.24 = (f32[2,2,4,64]{3,2,1,0:T(4,128)S(1)}, f32[2,2,4,64]{3,2,1,0:T(4,128)S(1)}, u32[]{:S(2)}, u32[]{:S(2)}) collective-permute-start(f32[2,2,4,64]{3,2,1,0:T(4,128)S(1)} %get-tuple-element.433), channel_id=1, source_target_pairs={{0,4},{4,8},{8,12},{12,16},{16,20},{20,24},{24,28},{28,32},{32,36}... | collective-permute-start | bytes 12296 | tf_op jit(solution)/shard_map/ppermute | solution.py:14
  227.9 22.0 %collective-permute-start.32 = (f32[1,4,64]{0,2,1:T(8,128)}, f32[1,4,64]{0,2,1:T(8,128)}, u32[]{:S(2)}, u32[]{:S(2)}) collective-permute-start(f32[1,4,64]{0,2,1:T(8,128)} %get-tuple-element.413), channel_id=1, source_target_pairs={{0,4},{4,8},{8,12},{12,16},{16,20},{20,24},{24,28},{28,32},{32,36}... | collective-permute-start | bytes 3080 | tf_op jit(solution)/shard_map/ppermute | solution.py:14
  235.9 15.1 %collective-permute-start.33 = (f32[1,4,64]{0,2,1:T(8,128)}, f32[1,4,64]{0,2,1:T(8,128)}, u32[]{:S(2)}, u32[]{:S(2)}) collective-permute-start(f32[1,4,64]{0,2,1:T(8,128)} %get-tuple-element.414), channel_id=1, source_target_pairs={{4,0},{8,4},{12,8},{16,12},{20,16},{24,20},{28,24},{32,28},{36,32}... | collective-permute-start | bytes 3080 | tf_op jit(solution)/shard_map/ppermute | solution.py:17
  238.4 99.6 %collective-permute-start.52 = (f32[1,2,32]{2,0,1:T(1,128)}, f32[1,2,32]{2,0,1:T(1,128)}, u32[]{:S(2)}, u32[]{:S(2)}) collective-permute-start(f32[1,2,32]{2,0,1:T(1,128)} %broadcast.368), channel_id=1, source_target_pairs={{0,4},{4,8},{8,12},{12,16},{16,20},{20,24},{24,28},{28,32},{32,36}... | collective-permute-start | bytes 776 | tf_op jit(solution)/shard_map/ppermute | solution.py:14
  245.3 92.7 %collective-permute-start.53 = (f32[1,2,32]{2,0,1:T(1,128)}, f32[1,2,32]{2,0,1:T(1,128)}, u32[]{:S(2)}, u32[]{:S(2)}) collective-permute-start(f32[1,2,32]{2,0,1:T(1,128)} %broadcast.368), channel_id=1, source_target_pairs={{4,0},{8,4},{12,8},{16,12},{20,16},{24,20},{28,24},{32,28},{36,32}... | collective-permute-start | bytes 776 | tf_op jit(solution)/shard_map/ppermute | solution.py:17
  262.3 12.6 %collective-permute-start.36 = (f32[1,4,64]{0,2,1:T(8,128)}, f32[1,4,64]{0,2,1:T(8,128)}, u32[]{:S(2)}, u32[]{:S(2)}) collective-permute-start(f32[1,4,64]{0,2,1:T(8,128)} %get-tuple-element.411), channel_id=1, source_target_pairs={{0,4},{4,8},{8,12},{12,16},{16,20},{20,24},{24,28},{28,32},{32,36}... | collective-permute-start | bytes 3080 | tf_op jit(solution)/shard_map/ppermute | solution.py:14
  270.7 9.9 collective-permute-start.37
  296.3 9.9 collective-permute-start.41
  322.5 9.9 collective-permute-start.45
  366.1 9.9 collective-permute-start.56
  754.2 9.9 collective-permute-start.89
  778.5 9.9 collective-permute-start.93
  802.9 9.9 collective-permute-start.97
  827.9 9.9 collective-permute-start.101
  853.5 13.8 %collective-permute-start.105 = (f32[1,8,128]{0,1,2:T(8,128)S(1)}, f32[1,8,128]{0,1,2:T(8,128)S(1)}, u32[]{:S(2)}, u32[]{:S(2)}) collective-permute-start(f32[1,8,128]{0,1,2:T(8,128)S(1)} %get-tuple-element.380), channel_id=1, source_target_pairs={{4,0},{8,4},{12,8},{16,12},{20,16},{24,20},{28,24},{32,28},{36,32}... | collective-permute-start | bytes 12296 | tf_op jit(solution)/shard_map/ppermute | solution.py:17
  881.6 13.8 %collective-permute-start.109 = (f32[1,8,128]{0,1,2:T(8,128)S(1)}, f32[1,8,128]{0,1,2:T(8,128)S(1)}, u32[]{:S(2)}, u32[]{:S(2)}) collective-permute-start(f32[1,8,128]{0,1,2:T(8,128)S(1)} %get-tuple-element.354), channel_id=1, source_target_pairs={{4,0},{8,4},{12,8},{16,12},{20,16},{24,20},{28,24},{32,28},{36,32}... | collective-permute-start | bytes 12296 | tf_op jit(solution)/shard_map/ppermute | solution.py:17
  909.6 13.8 %collective-permute-start.113 = (f32[1,8,128]{0,1,2:T(8,128)S(1)}, f32[1,8,128]{0,1,2:T(8,128)S(1)}, u32[]{:S(2)}, u32[]{:S(2)}) collective-permute-start(f32[1,8,128]{0,1,2:T(8,128)S(1)} %get-tuple-element.352), channel_id=1, source_target_pairs={{4,0},{8,4},{12,8},{16,12},{20,16},{24,20},{28,24},{32,28},{36,32}... | collective-permute-start | bytes 12296 | tf_op jit(solution)/shard_map/ppermute | solution.py:17
  937.4 13.8 %collective-permute-start.117 = (f32[1,8,128]{0,1,2:T(8,128)S(1)}, f32[1,8,128]{0,1,2:T(8,128)S(1)}, u32[]{:S(2)}, u32[]{:S(2)}) collective-permute-start(f32[1,8,128]{0,1,2:T(8,128)S(1)} %get-tuple-element.350), channel_id=1, source_target_pairs={{4,0},{8,4},{12,8},{16,12},{20,16},{24,20},{28,24},{32,28},{36,32}... | collective-permute-start | bytes 12296 | tf_op jit(solution)/shard_map/ppermute | solution.py:17
  965.2 13.8 %collective-permute-start.121 = (f32[1,8,128]{0,1,2:T(8,128)S(1)}, f32[1,8,128]{0,1,2:T(8,128)S(1)}, u32[]{:S(2)}, u32[]{:S(2)}) collective-permute-start(f32[1,8,128]{0,1,2:T(8,128)S(1)} %get-tuple-element.348), channel_id=1, source_target_pairs={{4,0},{8,4},{12,8},{16,12},{20,16},{24,20},{28,24},{32,28},{36,32}... | collective-permute-start | bytes 12296 | tf_op jit(solution)/shard_map/ppermute | solution.py:17
  (174 other events, 2344.0 us)
where the time goes:
time: 1010 us; the launch traced here: 994 us
  starting transfers between devices  301 us (30%)
  waiting for transfers between devices  267 us (26%)
  other arithmetic  231 us (23%)
  local copies, waits for them, and re-layouts  88.2 us (9%)
  blocking collectives  62.4 us (6%)
  loops' own time  40.1 us (4%)
    ppermute x62, waiting for transfers between devices, padded_2(): lax.ppermute(lax.slice_in_dim(block, 0, width, axis=dim), axis, backward)  236 us
    ppermute x62, starting transfers between devices, padded_2(): lax.ppermute(lax.slice_in_dim(block, block.shape[dim] - width, None, axis...  199 us
    ppermute x62, starting transfers between devices, padded_2(): lax.ppermute(lax.slice_in_dim(block, 0, width, axis=dim), axis, backward)  102 us
    all_gather x1, blocking collectives, local(): partial_grid = lax.all_gather(coarse, 'wide', axis=1, tiled=True)  53.1 us
    select_n x24, other arithmetic, smooth(): field = trimmed(jnp.where(inner_colour == parity, fresh, wider))  51.7 us
    reduce_sum x20, other arithmetic, advance(): alpha = norm_now / jnp.sum(search * image)  48.3 us
    another operation x1, loops' own time, bottom(): return lax.fori_loop(0, ITERS, advance, start)[0]  40.1 us
    ppermute x62, waiting for transfers between devices, padded_2(): lax.ppermute(lax.slice_in_dim(block, block.shape[dim] - width, None, axis...  31.3 us
  transfers between devices with their start and end apart: 124, of which 63 were waited for; matrix products, arithmetic and copies ran while one was open for 11% of the time, Pallas kernels for 0%

commit v1 on v0

v1 whole, which is shorter than its diff:
```python
import jax
import jax.numpy as jnp
from jax import lax
from jax.experimental import pallas as pl
from jax.experimental.pallas import tpu as pltpu
from jax.sharding import PartitionSpec as P

ITERS = 20
LANES = 128


class Level:
    def __init__(self, depth, pairs, rows, weights, beside):
        self.pairs, self.rows, self.step = pairs, rows, 1 << depth
        self.scale = 0.25**depth
        self.weights, self.beside = weights, beside
        z = lax.broadcasted_iota(jnp.int32, (rows, LANES), 0)
        lane = lax.broadcasted_iota(jnp.int32, (rows, LANES), 1)
        y = lane // self.step
        self.odd = (z + y) % 2 == 1
        self.y_odd = y % 2 == 1
        self.z_last, self.z_first = z == rows - 1, z == 0
        self.y_last, self.y_first = lane >= LANES - self.step, lane < self.step

    def other(self, colour, ref, i):
        after, before = ref[i + 1], ref[i - 1]
        return jnp.where(self.odd, after, before) if colour == 0 else jnp.where(self.odd, before, after)

    def rolled(self, value):
        return (
            pltpu.roll(value, self.rows - 1, 0),
            pltpu.roll(value, 1, 0),
            pltpu.roll(value, LANES - self.step, 1),
            pltpu.roll(value, self.step, 1),
        )

    def setup(self, conduct, low, high, first, count):
        edges = (self.z_last, self.z_first, self.y_last, self.y_first)

        def body(i):
            inside = jnp.logical_and(first + i >= 0, first + i < count)
            for colour in (0, 1):
                own, near = conduct[colour][i], conduct[1 - colour][i]
                same = 0.5 * (own + near)
                across = 0.5 * (own + self.other(colour, conduct[1 - colour], i))
                total = same + across
                if colour == 0:
                    self.beside[i] = same
                self.weights[colour, 0, i] = across
                for slot, (edge, value) in enumerate(zip(edges, self.rolled(near))):
                    face = 0.5 * (own + jnp.where(edge, 0.0, value))
                    total = total + face
                    self.weights[colour, 1 + slot, i] = jnp.where(edge, 0.0, face)
                self.weights[colour, 5, i] = total
                total = jnp.where(total > 0.0, total, 1.0)
                self.weights[colour, 6, i] = jnp.where(inside, 1.0 / total, 0.0)

        loop(low, high, body)

    def around(self, colour, field, i):
        near = field[1 - colour][i]
        total = self.beside[i] * near + self.weights[colour, 0, i] * self.other(colour, field[1 - colour], i)
        for slot, value in enumerate(self.rolled(near)):
            total = total + self.weights[colour, 1 + slot, i] * value
        return total

    def half(self, colour, field, source, low, high):
        def body(i):
            fresh = source[colour][i] + self.around(colour, field, i)
            field[colour][i] = fresh * self.weights[colour, 6, i]

        loop(low, high, body)

    def start(self, field, source, low, high):
        def body(i):
            field[0][i] = source[0][i] * self.weights[0, 6, i]

        loop(low, high, body)

    def defect(self, colour, field, source, i):
        rest = source[colour][i] + self.around(colour, field, i) - self.weights[colour, 5, i] * field[colour][i]
        return rest if self.scale == 1.0 else self.scale * rest

    def pair_sum(self, value):
        return value + jnp.where(self.y_odd, pltpu.roll(value, self.step, 1), pltpu.roll(value, LANES - self.step, 1))


def loop(low, high, body, group=2):
    whole = (high - low) // group * group
    if whole:

        def several(step, carry):
            for k in range(group):
                body(low + step * group + k)
            return carry

        lax.fori_loop(0, whole // group, several, 0)
    for i in range(low + whole, high):
        body(i)


def halved(ref, i, rows):
    return ref[i, pl.ds(0, rows // 2, 2), :] + ref[i, pl.ds(1, rows // 2, 2), :]


def zeroed(*refs):
    for ref in refs:
        ref[...] = jnp.zeros(ref.shape, ref.dtype)


def first_kernel(left, own, right, slab, one, two, weights0, beside0, weights1, beside1, buf1, sums, sums1, tmp):
    wide = lax.axis_index("wide")
    k0, f0, u0 = [(slab.at[2 * a], slab.at[2 * a + 1]) for a in range(3)]
    fine = Level(0, 24, 32, weights0, beside0)
    zeroed(u0[0])
    odd8 = fine.odd[:8]
    for base, part in ((0, left), (8, own), (16, right)):
        for n in range(4):
            z = slice(8 * n, 8 * n + 8)

            def unpack(i, part=part, n=n, z=z, base=base):
                for group, target in ((0, k0), (16, f0)):
                    even, uneven = part[n, group + 2 * i], part[n, group + 2 * i + 1]
                    target[0][base + i, z] = jnp.where(odd8, uneven, even)
                    target[1][base + i, z] = jnp.where(odd8, even, uneven)
                u0[1][base + i, z] = part[n, 32 + i]

            loop(0, 8, unpack)
    fine.setup(k0, 2, 22, 8 * wide - 8, 8 * lax.axis_size("wide"))
    fine.half(0, u0, f0, 2, 22)
    fine.half(1, u0, f0, 2, 22)
    fine.half(0, u0, f0, 3, 21)
    fine.half(1, u0, f0, 3, 21)

    def down_k(i):
        sums[i] = fine.pair_sum(k0[0][i] + k0[1][i])

    loop(2, 22, down_k)

    def down_f(i):
        sums1[i] = fine.pair_sum(fine.defect(0, u0, f0, i) + fine.defect(1, u0, f0, i))

    loop(4, 20, down_f)

    mid = Level(1, 12, 16, weights1, beside1)
    k1, f1, u1 = [(buf1.at[2 * a], buf1.at[2 * a + 1]) for a in range(3)]
    zeroed(u1[0], u1[1])

    def pack(target, source, factor, j):
        even, uneven = factor * halved(source, 2 * j, 32), factor * halved(source, 2 * j + 1, 32)
        target[0][j] = jnp.where(mid.odd, uneven, even)
        target[1][j] = jnp.where(mid.odd, even, uneven)

    loop(1, 11, lambda j: pack(k1, sums, 0.125, j))
    loop(2, 10, lambda j: pack(f1, sums1, 0.125 / 0.25, j))
    mid.setup(k1, 2, 10, 4 * wide - 4, 4 * lax.axis_size("wide"))
    mid.start(u1, f1, 2, 10)
    mid.half(1, u1, f1, 2, 10)
    mid.half(0, u1, f1, 3, 9)
    mid.half(1, u1, f1, 3, 9)
    for a in range(6):
        one[a] = buf1[a, 4:8]

    z8 = lax.broadcasted_iota(jnp.int32, (8, LANES), 0)
    lane8 = lax.broadcasted_iota(jnp.int32, (8, LANES), 1)
    odd2 = (z8 + lane8 // 4) % 2 == 1
    cells_k, cells_f = [], []
    for x in range(4):
        j = 4 + x
        tmp[2 * x] = mid.pair_sum(k1[0][j] + k1[1][j])
        tmp[2 * x + 1] = mid.pair_sum(mid.defect(0, u1, f1, j) + mid.defect(1, u1, f1, j))
        cells_k.append(0.125 * halved(tmp, 2 * x, 16))
        cells_f.append(0.125 / 0.0625 * halved(tmp, 2 * x + 1, 16))
    for t in range(2):
        for base, cells in ((0, cells_k), (2, cells_f)):
            even, uneven = cells[2 * t], cells[2 * t + 1]
            two[base, t] = jnp.where(odd2, uneven, even)
            two[base + 1, t] = jnp.where(odd2, even, uneven)


def second_kernel(*refs):
    parts, (slab, out, weights, beside) = refs[:7], refs[7:]
    wide = lax.axis_index("wide")
    level = Level(2, 16, 8, weights, beside)
    k, f, u = [(slab.at[2 * a], slab.at[2 * a + 1]) for a in range(3)]
    zeroed(slab)
    for place, part in enumerate(parts):
        for t in range(2):
            for a in range(4):
                slab[a, 1 + 2 * place + t] = part[a, t]
    level.setup(k, 1, 15, 2 * wide - 7, 2 * lax.axis_size("wide"))
    level.start(u, f, 1, 15)
    level.half(1, u, f, 2, 14)
    level.half(0, u, f, 2, 14)
    level.half(1, u, f, 3, 13)
    lane = lax.broadcasted_iota(jnp.int32, (8, LANES), 1)
    row = lax.broadcasted_iota(jnp.int32, (8, LANES), 0)
    pick = 8 * (lane % 16)
    keep = row == 2 * ((lane // 16) % 4)

    def compact(values):
        outs = []
        for value in values:
            value = level.pair_sum(value)
            value = 0.125 * (value + pltpu.roll(value, 7, 0))
            value = jnp.take_along_axis(value, pick, axis=1)
            outs.append(jnp.sum(jnp.where(keep, value, 0.0), axis=0, keepdims=True))
        return jnp.where(lane[:1] < 64, outs[0], outs[1])

    source = compact([level.defect(0, u, f, i) + level.defect(1, u, f, i) for i in (7, 8)])
    conduct = compact([k[0][i] + k[1][i] for i in (7, 8)])
    both = jnp.where(row % 2 == 0, source, conduct)
    for w in range(out.shape[0] // 8):
        out[8 * w : 8 * w + 8] = both


def coarsest(data, answer, remain, search, faces, iters):
    count = data.shape[0] // 2
    scale = 0.25**3
    row = lax.broadcasted_iota(jnp.int32, (count, LANES), 0)
    lane = lax.broadcasted_iota(jnp.int32, (count, LANES), 1)
    y, z, x = lane % 16, (lane // 16) % 4, lane // 64

    def around(value):
        swapped = pltpu.roll(value, 64, 1)
        across = jnp.where(x == 0, pltpu.roll(swapped, 1, 0), pltpu.roll(swapped, count - 1, 0))
        return (
            swapped,
            across,
            pltpu.roll(value, LANES - 16, 1),
            pltpu.roll(value, 16, 1),
            pltpu.roll(value, LANES - 1, 1),
            pltpu.roll(value, 1, 1),
        )

    source = data[pl.ds(0, count, 2), :]
    conduct = data[pl.ds(1, count, 2), :]
    edges = (
        None,
        jnp.logical_or(jnp.logical_and(x == 0, row == 0), jnp.logical_and(x == 1, row == count - 1)),
        z == 3,
        z == 0,
        y == 15,
        y == 0,
    )
    total = None
    for slot, (edge, value) in enumerate(zip(edges, around(conduct))):
        if edge is not None:
            value = jnp.where(edge, 0.0, value)
        face = (0.5 * scale) * (conduct + value)
        total = face if total is None else total + face
        faces[slot] = face if edge is None else jnp.where(edge, 0.0, face)
    faces[6] = total
    answer[...] = jnp.zeros_like(source)
    remain[...] = source
    search[...] = source

    def advance(step, norm):
        now = search[...]
        image = faces[6] * now
        for slot, value in enumerate(around(now)):
            image = image - faces[slot] * value
        alpha = norm / jnp.sum(now * image, axis=(0, 1), keepdims=True)
        answer[...] = answer[...] + alpha * now
        rest = remain[...] - alpha * image
        remain[...] = rest
        following = jnp.sum(rest * rest, axis=(0, 1), keepdims=True)
        search[...] = rest + (following / norm) * now
        return following

    lax.fori_loop(0, iters, advance, jnp.sum(source * source, axis=(0, 1), keepdims=True))


def third_kernel(data, slab2, left1, own1, right1, slab0, pressure, residual, answer, remain, search, faces,
                 weights2, beside2, u2, weights1, beside1, buf1, grow1, weights0, beside0, u0, grow0):
    wide, narrow = lax.axis_index("wide"), lax.axis_index("narrow")
    size = lax.axis_size("wide")
    zeroed(answer)
    coarsest(data, answer.at[pl.ds(8, data.shape[0] // 2)], remain, search, faces, ITERS)

    level = Level(2, 16, 8, weights2, beside2)
    k, f = [(slab2.at[2 * a], slab2.at[2 * a + 1]) for a in range(2)]
    zeroed(u2)
    lane = lax.broadcasted_iota(jnp.int32, (8, LANES), 1)
    row = lax.broadcasted_iota(jnp.int32, (8, LANES), 0)
    where_from = (row // 2) * 16 + lane // 8
    for t in range(5):
        line = answer[pl.ds(8 + wide - 2 + t, 1), :]
        line = jnp.broadcast_to(line, (8, LANES))
        for half in range(2):
            i = 3 + 2 * t + half
            u2[1, i] = slab2[5, i] + jnp.take_along_axis(line, where_from + 64 * half, axis=1)
    up2 = (u2.at[0], u2.at[1])
    level.setup(k, 3, 13, 2 * wide - 7, 2 * size)
    level.half(0, up2, f, 3, 13)
    level.half(1, up2, f, 4, 12)
    level.half(0, up2, f, 4, 12)
    level.half(1, up2, f, 5, 11)

    mid = Level(1, 12, 16, weights1, beside1)
    k1, f1, u1 = [(buf1.at[2 * a], buf1.at[2 * a + 1]) for a in range(3)]
    zeroed(u1[0])
    for a in (0, 1, 2, 3, 5):
        for place, part in enumerate((left1, own1, right1)):
            buf1[a, 4 * place : 4 * place + 4] = part[a]
    for j in range(12):
        i, side = 5 + j // 2, j % 2
        cell = jnp.where(level.odd, up2[1 - side][i], up2[side][i])
        grow1[j, pl.ds(0, 8, 2), :] = cell
        grow1[j, pl.ds(1, 8, 2), :] = cell
    for j in range(12):
        u1[1][j] = u1[1][j] + grow1[j]
    mid.setup(k1, 1, 11, 4 * wide - 4, 4 * size)
    mid.half(0, u1, f1, 1, 11)
    mid.half(1, u1, f1, 1, 11)
    mid.half(0, u1, f1, 2, 10)
    mid.half(1, u1, f1, 2, 10)

    fine = Level(0, 24, 32, weights0, beside0)
    k0, f0 = [(slab0.at[2 * a], slab0.at[2 * a + 1]) for a in range(2)]
    zeroed(u0.at[0])
    for i in range(5, 19):
        j, side = (i - 8 + 8) // 2, i % 2
        cell = jnp.where(mid.odd, u1[1 - side][j], u1[side][j])
        grow0[i, pl.ds(0, 16, 2), :] = cell
        grow0[i, pl.ds(1, 16, 2), :] = cell
    for i in range(5, 19):
        u0[1, i] = slab0[5, i] + grow0[i]
    up0 = (u0.at[0], u0.at[1])
    fine.setup(k0, 6, 18, 8 * wide - 8, 8 * size)
    fine.half(0, up0, f0, 6, 18)
    fine.half(1, up0, f0, 6, 18)
    fine.half(0, up0, f0, 7, 17)
    fine.half(1, up0, f0, 7, 17)
    odd8 = fine.odd[:8]

    def finish(i):
        grow0[0] = fine.defect(0, up0, f0, i)
        grow0[1] = fine.defect(1, up0, f0, i)
        rows = pl.ds(pl.multiple_of(8 * narrow, 8), 8)
        for out, first, second in (
            (pressure, u0[0, i, rows, :], u0[1, i, rows, :]),
            (residual, grow0[0, rows, :], grow0[1, rows, :]),
        ):
            out[2 * (i - 8)] = jnp.where(odd8, second, first)
            out[2 * (i - 8) + 1] = jnp.where(odd8, first, second)

    loop(8, 16, finish, group=1)


def f32(*shape):
    return jax.ShapeDtypeStruct(shape, jnp.float32)


def scratch(*shape):
    return pltpu.VMEM(shape, jnp.float32)


PARAMS = pltpu.CompilerParams(vmem_limit_bytes=48 * 1024 * 1024)


def shifted(block, distance):
    count = lax.axis_size("wide")
    if distance > 0:
        pairs = [(i, i + distance) for i in range(count - distance)]
    else:
        pairs = [(i, i + distance) for i in range(-distance, count)]
    return lax.ppermute(block, "wide", pairs)


def local(rhs, coefficient, guess):
    shape = (8, 8, LANES)
    odd = (lax.broadcasted_iota(jnp.int32, shape, 1) + lax.broadcasted_iota(jnp.int32, shape, 2)) % 2 == 1
    packed = jnp.where(odd, guess[0::2], guess[1::2])
    block = jnp.concatenate([coefficient, rhs, packed], axis=0)
    whole = lax.all_gather(block, "narrow")
    left, right = shifted(whole, 1), shifted(whole, -1)
    slab0, one, two = pl.pallas_call(
        first_kernel,
        out_shape=(f32(6, 24, 32, LANES), f32(6, 4, 16, LANES), f32(4, 2, 8, LANES)),
        scratch_shapes=[
            scratch(2, 7, 24, 32, LANES),
            scratch(24, 32, LANES),
            scratch(2, 7, 12, 16, LANES),
            scratch(12, 16, LANES),
            scratch(6, 12, 16, LANES),
            scratch(24, 32, LANES),
            scratch(24, 32, LANES),
            scratch(8, 16, LANES),
        ],
        compiler_params=PARAMS,
        name="first",
    )(left, whole, right)
    parts2 = [two if d == 0 else shifted(two, d) for d in (3, 2, 1, 0, -1, -2, -3)]
    left1, right1 = shifted(one, 1), shifted(one, -1)
    count = lax.axis_size("wide")
    slab2, out3 = pl.pallas_call(
        second_kernel,
        out_shape=(f32(6, 16, 8, LANES), f32(2 * count, LANES)),
        scratch_shapes=[scratch(2, 7, 16, 8, LANES), scratch(16, 8, LANES)],
        compiler_params=PARAMS,
        name="second",
    )(*parts2)
    data = lax.all_to_all(out3.reshape(count, 2, LANES), "wide", 0, 0).reshape(2 * count, LANES)
    return pl.pallas_call(
        third_kernel,
        out_shape=(f32(16, 8, LANES), f32(16, 8, LANES)),
        scratch_shapes=[
            scratch(count + 16, LANES),
            scratch(count, LANES),
            scratch(count, LANES),
            scratch(7, count, LANES),
            scratch(2, 7, 16, 8, LANES),
            scratch(16, 8, LANES),
            scratch(2, 16, 8, LANES),
            scratch(2, 7, 12, 16, LANES),
            scratch(12, 16, LANES),
            scratch(6, 12, 16, LANES),
            scratch(12, 16, LANES),
            scratch(2, 7, 24, 32, LANES),
            scratch(24, 32, LANES),
            scratch(2, 24, 32, LANES),
            scratch(24, 32, LANES),
        ],
        compiler_params=PARAMS,
        name="third",
    )(data, slab2, left1, one, right1, slab0)


def solution(mesh):
    spec = P("wide", "narrow", None)
    return jax.shard_map(
        local, mesh=mesh, in_specs=(spec, spec, spec), out_specs=(spec, spec), check_vma=False
    )
```

time: 1010 us -> 110 us (0.11)
  the two profiles are of different devices: /device:TPU:249 before, /device:TPU:1 now
where the time goes in v1:
time: 110 us
  starting transfers between devices  52.3 us (48%)
  Pallas kernels  28.1 us (26%)
  waiting for transfers between devices  15.6 us (14%)
  blocking collectives  11.3 us (10%)
  other arithmetic  1.67 us (2%)
    ppermute x10, starting transfers between devices, shifted(): return lax.ppermute(block, 'wide', pairs)  35.2 us
    all_to_all x1, starting transfers between devices, local(): lax.all_to_all(out3.reshape(count, 2, LANES), 'wide', 0, 0)  17.1 us
    pallas_call x1, Pallas kernels, local(): pl.pallas_call(third_kernel, out_shape=(f32(16, 8, LANES), f32(16, 8, LAN...  16.6 us
    all_gather x1, blocking collectives, local(): whole = lax.all_gather(block, 'narrow')  11.3 us
    ppermute x10, waiting for transfers between devices, shifted(): return lax.ppermute(block, 'wide', pairs)  11.1 us
    pallas_call x1, Pallas kernels, local(): pl.pallas_call(first_kernel, out_shape=(f32(6, 24, 32, LANES), f32(6, 4,...  8.65 us
    all_to_all x1, waiting for transfers between devices, local(): lax.all_to_all(out3.reshape(count, 2, LANES), 'wide', 0, 0)  4.56 us
    pallas_call x1, Pallas kernels, local(): pl.pallas_call(second_kernel, out_shape=(f32(6, 16, 8, LANES), f32(2 * co...  2.88 us
  transfers between devices with their start and end apart: 11, of which 6 were waited for; matrix products, arithmetic and copies ran while one was open for 0% of the time, Pallas kernels for 0%

profile of v1, /device:TPU:1, one launch (start us, length us, event | category | flops | bytes accessed | tf_op | source)
XLA Modules:
  0.0 109.9 jit_solution(5236555066119224177)
XLA Ops:
  0.6 0.8 slice_select_fusion
  1.4 0.9 pad_maximum_fusion
  2.3 11.3 %all-gather = f32[160,8,128]{2,1,0:T(8,128)S(1)} all-gather(f32[40,8,128]{2,1,0:T(8,128)S(1)} %pad_maximum_fusion), channel_id=2, replica_groups=mesh['wide'=128,'narrow'=4] {'narrow'}, dimensions={0}, use_global_device_ids=true | all-gather | bytes 819200 | tf_op jit(solution)/shard_map/all_gather | solution.py:376
  13.6 10.5 %collective-permute-start.1 = (f32[4,40,8,128]{3,2,1,0:T(8,128)S(1)}, f32[4,40,8,128]{3,2,1,0:T(8,128)S(1)}, u32[]{:S(2)}, u32[]{:S(2)}) collective-permute-start(f32[4,40,8,128]{3,2,1,0:T(8,128)S(1)} %bitcast.3), channel_id=1, source_target_pairs={{4,0},{8,4},{12,8},{16,12},{20,16},{24,20},{28,24},{32,28},{36,32}... | collective-permute-start | bytes 1966088 | tf_op jit(solution)/shard_map/ppermute | solution.py:368
  24.1 1.9 %collective-permute-start = (f32[4,40,8,128]{3,2,1,0:T(8,128)S(1)}, f32[4,40,8,128]{3,2,1,0:T(8,128)S(1)}, u32[]{:S(2)}, u32[]{:S(2)}) collective-permute-start(f32[4,40,8,128]{3,2,1,0:T(8,128)S(1)} %bitcast.4), channel_id=1, source_target_pairs={{0,4},{4,8},{8,12},{12,16},{16,20},{20,24},{24,28},{28,32},{32,36}... | collective-permute-start | bytes 1966088 | tf_op jit(solution)/shard_map/ppermute | solution.py:368
  26.1 2.5 %collective-permute-done.1.right = f32[4,40,8,128]{3,2,1,0:T(8,128)S(1)} collective-permute-done((f32[4,40,8,128]{3,2,1,0:T(8,128)S(1)}, f32[4,40,8,128]{3,2,1,0:T(8,128)S(1)}, u32[]{:S(2)}, u32[]{:S(2)}) %collective-permute-start.1) | collective-permute-done | bytes 655392 | tf_op jit(solution)/shard_map/ppermute | solution.py:368
  28.5 5.0 %collective-permute-done.left = f32[4,40,8,128]{3,2,1,0:T(8,128)S(1)} collective-permute-done((f32[4,40,8,128]{3,2,1,0:T(8,128)S(1)}, f32[4,40,8,128]{3,2,1,0:T(8,128)S(1)}, u32[]{:S(2)}, u32[]{:S(2)}) %collective-permute-start) | collective-permute-done | bytes 655392 | tf_op jit(solution)/shard_map/ppermute | solution.py:368
  33.6 8.7 %first.1 = (f32[6,24,32,128]{3,2,1,0:T(8,128)S(1)}, f32[6,4,16,128]{3,2,1,0:T(8,128)S(1)}, f32[4,2,8,128]{3,2,1,0:T(8,128)S(1)}) custom-call(f32[4,40,8,128]{3,2,1,0:T(8,128)S(1)} %collective-permute-done.left, f32[4,40,8,128]{3,2,1,0:T(8,128)S(1)} %bitcast.5, f32[4,40,8,128]{3,2,1,0:T(8,128)S(1)} %collective-permute-done.1.right), custom_call_target="tpu_custom_call" | custom-call | tf_op jit(solution)/shard_map/first/pallas_call | solution.py:378
  42.2 1.3 %collective-permute-start.7 = (f32[4,2,8,128]{3,2,1,0:T(8,128)S(1)}, f32[4,2,8,128]{3,2,1,0:T(8,128)S(1)}, u32[]{:S(2)}, u32[]{:S(2)}) collective-permute-start(f32[4,2,8,128]{3,2,1,0:T(8,128)S(1)} %get-tuple-element.7.refs_3_), channel_id=1, source_target_pairs={{12,0},{16,4},{20,8},{24,12},{28,16},{32,20},{36,24},{40,28},{44,3... | collective-permute-start | bytes 98312 | tf_op jit(solution)/shard_map/ppermute | solution.py:368
  43.5 1.3 %collective-permute-start.6 = (f32[4,2,8,128]{3,2,1,0:T(8,128)S(1)}, f32[4,2,8,128]{3,2,1,0:T(8,128)S(1)}, u32[]{:S(2)}, u32[]{:S(2)}) collective-permute-start(f32[4,2,8,128]{3,2,1,0:T(8,128)S(1)} %get-tuple-element.7.refs_3_), channel_id=1, source_target_pairs={{8,0},{12,4},{16,8},{20,12},{24,16},{28,20},{32,24},{36,28},{40,32... | collective-permute-start | bytes 98312 | tf_op jit(solution)/shard_map/ppermute | solution.py:368
  44.8 1.9 %collective-permute-start.5 = (f32[4,2,8,128]{3,2,1,0:T(8,128)S(1)}, f32[4,2,8,128]{3,2,1,0:T(8,128)S(1)}, u32[]{:S(2)}, u32[]{:S(2)}) collective-permute-start(f32[4,2,8,128]{3,2,1,0:T(8,128)S(1)} %get-tuple-element.7.refs_3_), channel_id=1, source_target_pairs={{4,0},{8,4},{12,8},{16,12},{20,16},{24,20},{28,24},{32,28},{36,32}... | collective-permute-start | bytes 98312 | tf_op jit(solution)/shard_map/ppermute | solution.py:368
  46.8 5.0 %collective-permute-start.4 = (f32[4,2,8,128]{3,2,1,0:T(8,128)S(1)}, f32[4,2,8,128]{3,2,1,0:T(8,128)S(1)}, u32[]{:S(2)}, u32[]{:S(2)}) collective-permute-start(f32[4,2,8,128]{3,2,1,0:T(8,128)S(1)} %get-tuple-element.7.refs_3_), channel_id=1, source_target_pairs={{0,4},{4,8},{8,12},{12,16},{16,20},{20,24},{24,28},{28,32},{32,36}... | collective-permute-start | bytes 98312 | tf_op jit(solution)/shard_map/ppermute | solution.py:368
  51.8 3.6 %collective-permute-start.3 = (f32[4,2,8,128]{3,2,1,0:T(8,128)S(1)}, f32[4,2,8,128]{3,2,1,0:T(8,128)S(1)}, u32[]{:S(2)}, u32[]{:S(2)}) collective-permute-start(f32[4,2,8,128]{3,2,1,0:T(8,128)S(1)} %get-tuple-element.7.refs_3_), channel_id=1, source_target_pairs={{0,8},{4,12},{8,16},{12,20},{16,24},{20,28},{24,32},{28,36},{32,40... | collective-permute-start | bytes 98312 | tf_op jit(solution)/shard_map/ppermute | solution.py:368
  55.4 0.0 collective-permute-done.7.refs_6_
  55.4 4.1 %collective-permute-start.2 = (f32[4,2,8,128]{3,2,1,0:T(8,128)S(1)}, f32[4,2,8,128]{3,2,1,0:T(8,128)S(1)}, u32[]{:S(2)}, u32[]{:S(2)}) collective-permute-start(f32[4,2,8,128]{3,2,1,0:T(8,128)S(1)} %get-tuple-element.7.refs_3_), channel_id=1, source_target_pairs={{0,12},{4,16},{8,20},{12,24},{16,28},{20,32},{24,36},{28,40},{32,4... | collective-permute-start | bytes 98312 | tf_op jit(solution)/shard_map/ppermute | solution.py:368
  59.5 0.0 collective-permute-done.6.refs_5_
  59.6 0.0 collective-permute-done.5.refs_4_
  59.6 0.0 collective-permute-done.4.refs_2_
  59.6 0.0 collective-permute-done.3.refs_1_
  59.6 1.0 collective-permute-done.2.refs_0_
  60.6 2.9 %second.1 = (f32[6,16,8,128]{3,2,1,0:T(8,128)S(1)}, f32[256,128]{1,0:T(8,128)}) custom-call(f32[4,2,8,128]{3,2,1,0:T(8,128)S(1)} %collective-permute-done.2.refs_0_, f32[4,2,8,128]{3,2,1,0:T(8,128)S(1)} %collective-permute-done.3.refs_1_, f32[4,2,8,128]{3,2,1,0:T(8,128)S(1)} %collective-permute-done.4.refs_2_, ...), custom_call_target="tpu_custom_call" | custom-call | tf_op jit(solution)/shard_map/second/pallas_call | solution.py:397
  63.4 17.1 %all-to-all-start = ((f32[128,2,128]{2,1,0:T(2,128)}), f32[128,2,128]{2,1,0:T(2,128)S(1)}, u32[]{:S(2)}, u32[]{:S(2)}) async-start(f32[128,2,128]{2,1,0:T(2,128)} %bitcast.1), calls=%async_computation | async-start | bytes 262144 | tf_op jit(solution)/shard_map/all_to_all | solution.py:404
  80.6 2.8 %collective-permute-start.9 = (f32[6,4,16,128]{3,2,1,0:T(8,128)S(1)}, f32[6,4,16,128]{3,2,1,0:T(8,128)S(1)}, u32[]{:S(2)}, u32[]{:S(2)}) collective-permute-start(f32[6,4,16,128]{3,2,1,0:T(8,128)S(1)} %get-tuple-element.10.own1), channel_id=1, source_target_pairs={{4,0},{8,4},{12,8},{16,12},{20,16},{24,20},{28,24},{32,28},{36,32}... | collective-permute-start | bytes 589832 | tf_op jit(solution)/shard_map/ppermute | solution.py:368
  83.4 2.8 %collective-permute-start.8 = (f32[6,4,16,128]{3,2,1,0:T(8,128)S(1)}, f32[6,4,16,128]{3,2,1,0:T(8,128)S(1)}, u32[]{:S(2)}, u32[]{:S(2)}) collective-permute-start(f32[6,4,16,128]{3,2,1,0:T(8,128)S(1)} %get-tuple-element.10.own1), channel_id=1, source_target_pairs={{0,4},{4,8},{8,12},{12,16},{16,20},{20,24},{24,28},{28,32},{32,36}... | collective-permute-start | bytes 589832 | tf_op jit(solution)/shard_map/ppermute | solution.py:368
  86.1 1.7 %collective-permute-done.9.right1 = f32[6,4,16,128]{3,2,1,0:T(8,128)S(1)} collective-permute-done((f32[6,4,16,128]{3,2,1,0:T(8,128)S(1)}, f32[6,4,16,128]{3,2,1,0:T(8,128)S(1)}, u32[]{:S(2)}, u32[]{:S(2)}) %collective-permute-start.9) | collective-permute-done | bytes 196640 | tf_op jit(solution)/shard_map/ppermute | solution.py:368
  87.9 0.9 collective-permute-done.8.left1
  88.7 4.6 %all-to-all-done = f32[128,2,128]{2,1,0:T(2,128)S(1)} async-done(((f32[128,2,128]{2,1,0:T(2,128)}), f32[128,2,128]{2,1,0:T(2,128)S(1)}, u32[]{:S(2)}, u32[]{:S(2)}) %all-to-all-start) | async-done | bytes 131104 | tf_op jit(solution)/shard_map/all_to_all | solution.py:404
  93.3 16.6 %third.1 = (f32[16,8,128]{2,1,0:T(8,128)}, f32[16,8,128]{2,1,0:T(8,128)}) custom-call(f32[256,128]{1,0:T(8,128)S(1)} %bitcast.6, f32[6,16,8,128]{3,2,1,0:T(8,128)S(1)} %get-tuple-element.9.slab2, f32[6,4,16,128]{3,2,1,0:T(8,128)S(1)} %collective-permute-done.8.left1, f32[6,4,16,128]{3,2,1,0:T(8,128)S(1)} %get-tuple-element.10.own1, ...), custom_call_target="tpu_custom_call" | custom-call | tf_op jit(solution)/shard_map/third/pallas_call | solution.py:405
Async XLA Ops:
  13.6 14.9 %collective-permute-start.1 = (f32[4,40,8,128]{3,2,1,0:T(8,128)S(1)}, f32[4,40,8,128]{3,2,1,0:T(8,128)S(1)}, u32[]{:S(2)}, u32[]{:S(2)}) collective-permute-start(f32[4,40,8,128]{3,2,1,0:T(8,128)S(1)} %bitcast.3), channel_id=1, source_target_pairs={{4,0},{8,4},{12,8},{16,12},{20,16},{24,20},{28,24},{32,28},{36,32}... | collective-permute-start | bytes 1966088 | tf_op jit(solution)/shard_map/ppermute | solution.py:368
  24.1 9.4 %collective-permute-start = (f32[4,40,8,128]{3,2,1,0:T(8,128)S(1)}, f32[4,40,8,128]{3,2,1,0:T(8,128)S(1)}, u32[]{:S(2)}, u32[]{:S(2)}) collective-permute-start(f32[4,40,8,128]{3,2,1,0:T(8,128)S(1)} %bitcast.4), channel_id=1, source_target_pairs={{0,4},{4,8},{8,12},{12,16},{16,20},{20,24},{24,28},{28,32},{32,36}... | collective-permute-start | bytes 1966088 | tf_op jit(solution)/shard_map/ppermute | solution.py:368
  42.2 13.2 %collective-permute-start.7 = (f32[4,2,8,128]{3,2,1,0:T(8,128)S(1)}, f32[4,2,8,128]{3,2,1,0:T(8,128)S(1)}, u32[]{:S(2)}, u32[]{:S(2)}) collective-permute-start(f32[4,2,8,128]{3,2,1,0:T(8,128)S(1)} %get-tuple-element.7.refs_3_), channel_id=1, source_target_pairs={{12,0},{16,4},{20,8},{24,12},{28,16},{32,20},{36,24},{40,28},{44,3... | collective-permute-start | bytes 98312 | tf_op jit(solution)/shard_map/ppermute | solution.py:368
  43.5 16.0 %collective-permute-start.6 = (f32[4,2,8,128]{3,2,1,0:T(8,128)S(1)}, f32[4,2,8,128]{3,2,1,0:T(8,128)S(1)}, u32[]{:S(2)}, u32[]{:S(2)}) collective-permute-start(f32[4,2,8,128]{3,2,1,0:T(8,128)S(1)} %get-tuple-element.7.refs_3_), channel_id=1, source_target_pairs={{8,0},{12,4},{16,8},{20,12},{24,16},{28,20},{32,24},{36,28},{40,32... | collective-permute-start | bytes 98312 | tf_op jit(solution)/shard_map/ppermute | solution.py:368
  44.8 14.7 %collective-permute-start.5 = (f32[4,2,8,128]{3,2,1,0:T(8,128)S(1)}, f32[4,2,8,128]{3,2,1,0:T(8,128)S(1)}, u32[]{:S(2)}, u32[]{:S(2)}) collective-permute-start(f32[4,2,8,128]{3,2,1,0:T(8,128)S(1)} %get-tuple-element.7.refs_3_), channel_id=1, source_target_pairs={{4,0},{8,4},{12,8},{16,12},{20,16},{24,20},{28,24},{32,28},{36,32}... | collective-permute-start | bytes 98312 | tf_op jit(solution)/shard_map/ppermute | solution.py:368
  46.8 12.8 %collective-permute-start.4 = (f32[4,2,8,128]{3,2,1,0:T(8,128)S(1)}, f32[4,2,8,128]{3,2,1,0:T(8,128)S(1)}, u32[]{:S(2)}, u32[]{:S(2)}) collective-permute-start(f32[4,2,8,128]{3,2,1,0:T(8,128)S(1)} %get-tuple-element.7.refs_3_), channel_id=1, source_target_pairs={{0,4},{4,8},{8,12},{12,16},{16,20},{20,24},{24,28},{28,32},{32,36}... | collective-permute-start | bytes 98312 | tf_op jit(solution)/shard_map/ppermute | solution.py:368
  51.8 7.8 %collective-permute-start.3 = (f32[4,2,8,128]{3,2,1,0:T(8,128)S(1)}, f32[4,2,8,128]{3,2,1,0:T(8,128)S(1)}, u32[]{:S(2)}, u32[]{:S(2)}) collective-permute-start(f32[4,2,8,128]{3,2,1,0:T(8,128)S(1)} %get-tuple-element.7.refs_3_), channel_id=1, source_target_pairs={{0,8},{4,12},{8,16},{12,20},{16,24},{20,28},{24,32},{28,36},{32,40... | collective-permute-start | bytes 98312 | tf_op jit(solution)/shard_map/ppermute | solution.py:368
  55.4 5.1 %collective-permute-start.2 = (f32[4,2,8,128]{3,2,1,0:T(8,128)S(1)}, f32[4,2,8,128]{3,2,1,0:T(8,128)S(1)}, u32[]{:S(2)}, u32[]{:S(2)}) collective-permute-start(f32[4,2,8,128]{3,2,1,0:T(8,128)S(1)} %get-tuple-element.7.refs_3_), channel_id=1, source_target_pairs={{0,12},{4,16},{8,20},{12,24},{16,28},{20,32},{24,36},{28,40},{32,4... | collective-permute-start | bytes 98312 | tf_op jit(solution)/shard_map/ppermute | solution.py:368
  63.4 29.8 %all-to-all-start = ((f32[128,2,128]{2,1,0:T(2,128)}), f32[128,2,128]{2,1,0:T(2,128)S(1)}, u32[]{:S(2)}, u32[]{:S(2)}) async-start(f32[128,2,128]{2,1,0:T(2,128)} %bitcast.1), calls=%async_computation | async-start | bytes 262144 | tf_op jit(solution)/shard_map/all_to_all | solution.py:404
  80.6 7.3 %collective-permute-start.9 = (f32[6,4,16,128]{3,2,1,0:T(8,128)S(1)}, f32[6,4,16,128]{3,2,1,0:T(8,128)S(1)}, u32[]{:S(2)}, u32[]{:S(2)}) collective-permute-start(f32[6,4,16,128]{3,2,1,0:T(8,128)S(1)} %get-tuple-element.10.own1), channel_id=1, source_target_pairs={{4,0},{8,4},{12,8},{16,12},{20,16},{24,20},{28,24},{32,28},{36,32}... | collective-permute-start | bytes 589832 | tf_op jit(solution)/shard_map/ppermute | solution.py:368
  83.4 5.4 %collective-permute-start.8 = (f32[6,4,16,128]{3,2,1,0:T(8,128)S(1)}, f32[6,4,16,128]{3,2,1,0:T(8,128)S(1)}, u32[]{:S(2)}, u32[]{:S(2)}) collective-permute-start(f32[6,4,16,128]{3,2,1,0:T(8,128)S(1)} %get-tuple-element.10.own1), channel_id=1, source_target_pairs={{0,4},{4,8},{8,12},{12,16},{16,20},{20,24},{24,28},{28,32},{32,36}... | collective-permute-start | bytes 589832 | tf_op jit(solution)/shard_map/ppermute | solution.py:368

commit v2 on v1

--- a/solution.py
+++ b/solution.py
@@ -19,6 +19,7 @@
         y = lane // self.step
         self.odd = (z + y) % 2 == 1
         self.y_odd = y % 2 == 1
+        self.y_odd_lane = lane % 2 == 1
         self.z_last, self.z_first = z == rows - 1, z == 0
         self.y_last, self.y_first = lane >= LANES - self.step, lane < self.step
 
@@ -85,7 +86,7 @@
         return value + jnp.where(self.y_odd, pltpu.roll(value, self.step, 1), pltpu.roll(value, LANES - self.step, 1))
 
 
-def loop(low, high, body, group=2):
+def loop(low, high, body, group=20):
     whole = (high - low) // group * group
     if whole:
 
@@ -108,7 +109,7 @@
         ref[...] = jnp.zeros(ref.shape, ref.dtype)
 
 
-def first_kernel(left, own, right, slab, one, two, weights0, beside0, weights1, beside1, buf1, sums, sums1, tmp):
+def first_kernel(left, own, right, slab, send, weights0, beside0, weights1, beside1, buf1, sums, sums1, tmp):
     wide = lax.axis_index("wide")
     k0, f0, u0 = [(slab.at[2 * a], slab.at[2 * a + 1]) for a in range(3)]
     fine = Level(0, 24, 32, weights0, beside0)
@@ -158,41 +159,54 @@
     mid.half(1, u1, f1, 2, 10)
     mid.half(0, u1, f1, 3, 9)
     mid.half(1, u1, f1, 3, 9)
-    for a in range(6):
-        one[a] = buf1[a, 4:8]
+    for slot, a in enumerate((0, 1, 2, 3, 5)):
+        for t in range(2):
+            both = jnp.where(mid.y_odd_lane, buf1[a, 5 + 2 * t], buf1[a, 4 + 2 * t])
+            send[4 * slot + 2 * t : 4 * slot + 2 * t + 2] = both.reshape(2, 8, LANES)
 
     z8 = lax.broadcasted_iota(jnp.int32, (8, LANES), 0)
     lane8 = lax.broadcasted_iota(jnp.int32, (8, LANES), 1)
     odd2 = (z8 + lane8 // 4) % 2 == 1
-    cells_k, cells_f = [], []
+
+    def write(base, cells):
+        for t in range(len(cells) // 2):
+            even, uneven = cells[2 * t], cells[2 * t + 1]
+            send[base + t] = jnp.where(odd2, uneven, even)
+            send[base + len(cells) // 2 + t] = jnp.where(odd2, even, uneven)
+
+    for x in range(8):
+        tmp[x] = mid.pair_sum(k1[0][2 + x] + k1[1][2 + x])
     for x in range(4):
         j = 4 + x
-        tmp[2 * x] = mid.pair_sum(k1[0][j] + k1[1][j])
-        tmp[2 * x + 1] = mid.pair_sum(mid.defect(0, u1, f1, j) + mid.defect(1, u1, f1, j))
-        cells_k.append(0.125 * halved(tmp, 2 * x, 16))
-        cells_f.append(0.125 / 0.0625 * halved(tmp, 2 * x + 1, 16))
-    for t in range(2):
-        for base, cells in ((0, cells_k), (2, cells_f)):
-            even, uneven = cells[2 * t], cells[2 * t + 1]
-            two[base, t] = jnp.where(odd2, uneven, even)
-            two[base + 1, t] = jnp.where(odd2, even, uneven)
-
-
-def second_kernel(*refs):
-    parts, (slab, out, weights, beside) = refs[:7], refs[7:]
+        tmp[8 + x] = mid.pair_sum(mid.defect(0, u1, f1, j) + mid.defect(1, u1, f1, j))
+    write(20, [0.125 * halved(tmp, x, 16) for x in range(8)])
+    write(28, [0.125 / 0.0625 * halved(tmp, 8 + x, 16) for x in range(4)])
+
+
+def place_two(slab, part, base):
+    for c in range(2):
+        for t in range(4):
+            slab[c, base - 1 + t] = part[20 + 4 * c + t]
+        for t in range(2):
+            slab[2 + c, base + t] = part[28 + 2 * c + t]
+
+
+def second_kernel(left, own, right, out, near_low, near_high, slab, weights, beside):
     wide = lax.axis_index("wide")
     level = Level(2, 16, 8, weights, beside)
     k, f, u = [(slab.at[2 * a], slab.at[2 * a + 1]) for a in range(3)]
     zeroed(slab)
-    for place, part in enumerate(parts):
-        for t in range(2):
-            for a in range(4):
-                slab[a, 1 + 2 * place + t] = part[a, t]
-    level.setup(k, 1, 15, 2 * wide - 7, 2 * lax.axis_size("wide"))
-    level.start(u, f, 1, 15)
-    level.half(1, u, f, 2, 14)
-    level.half(0, u, f, 2, 14)
-    level.half(1, u, f, 3, 13)
+    place_two(slab, left, 5)
+    place_two(slab, right, 9)
+    place_two(slab, own, 7)
+    for a in range(4):
+        near_high[a] = slab[a, 5:9]
+        near_low[a] = slab[a, 7:11]
+    level.setup(k, 5, 11, 2 * wide - 7, 2 * lax.axis_size("wide"))
+    level.start(u, f, 5, 11)
+    level.half(1, u, f, 5, 11)
+    level.half(0, u, f, 6, 10)
+    level.half(1, u, f, 6, 10)
     lane = lax.broadcasted_iota(jnp.int32, (8, LANES), 1)
     row = lax.broadcasted_iota(jnp.int32, (8, LANES), 0)
     pick = 8 * (lane % 16)
@@ -214,84 +228,125 @@
         out[8 * w : 8 * w + 8] = both
 
 
-def coarsest(data, answer, remain, search, faces, iters):
-    count = data.shape[0] // 2
+def coarsest(data, answer, remain, search, image, faces, iters):
+    parts = data.shape[0] // 16
     scale = 0.25**3
-    row = lax.broadcasted_iota(jnp.int32, (count, LANES), 0)
-    lane = lax.broadcasted_iota(jnp.int32, (count, LANES), 1)
+    row = lax.broadcasted_iota(jnp.int32, (8, LANES), 0)
+    lane = lax.broadcasted_iota(jnp.int32, (8, LANES), 1)
     y, z, x = lane % 16, (lane // 16) % 4, lane // 64
 
-    def around(value):
-        swapped = pltpu.roll(value, 64, 1)
-        across = jnp.where(x == 0, pltpu.roll(swapped, 1, 0), pltpu.roll(swapped, count - 1, 0))
-        return (
-            swapped,
-            across,
-            pltpu.roll(value, LANES - 16, 1),
-            pltpu.roll(value, 16, 1),
-            pltpu.roll(value, LANES - 1, 1),
-            pltpu.roll(value, 1, 1),
-        )
-
-    source = data[pl.ds(0, count, 2), :]
-    conduct = data[pl.ds(1, count, 2), :]
-    edges = (
-        None,
-        jnp.logical_or(jnp.logical_and(x == 0, row == 0), jnp.logical_and(x == 1, row == count - 1)),
-        z == 3,
-        z == 0,
-        y == 15,
-        y == 0,
-    )
-    total = None
-    for slot, (edge, value) in enumerate(zip(edges, around(conduct))):
-        if edge is not None:
-            value = jnp.where(edge, 0.0, value)
-        face = (0.5 * scale) * (conduct + value)
-        total = face if total is None else total + face
-        faces[slot] = face if edge is None else jnp.where(edge, 0.0, face)
-    faces[6] = total
-    answer[...] = jnp.zeros_like(source)
-    remain[...] = source
-    search[...] = source
-
-    def advance(step, norm):
-        now = search[...]
-        image = faces[6] * now
-        for slot, value in enumerate(around(now)):
-            image = image - faces[slot] * value
-        alpha = norm / jnp.sum(now * image, axis=(0, 1), keepdims=True)
-        answer[...] = answer[...] + alpha * now
-        rest = remain[...] - alpha * image
-        remain[...] = rest
-        following = jnp.sum(rest * rest, axis=(0, 1), keepdims=True)
-        search[...] = rest + (following / norm) * now
-        return following
-
-    lax.fori_loop(0, iters, advance, jnp.sum(source * source, axis=(0, 1), keepdims=True))
-
-
-def third_kernel(data, slab2, left1, own1, right1, slab0, pressure, residual, answer, remain, search, faces,
-                 weights2, beside2, u2, weights1, beside1, buf1, grow1, weights0, beside0, u0, grow0):
+    def around(values):
+        swapped = [pltpu.roll(value, 64, 1) for value in values]
+        before = [pltpu.roll(swapped[-1], 1, 0)] + swapped[:-1]
+        after = swapped[1:] + [pltpu.roll(swapped[0], 7, 0)]
+        return [
+            (
+                swapped[v],
+                jnp.where(x == 0, before[v], after[v]),
+                pltpu.roll(value, LANES - 16, 1),
+                pltpu.roll(value, 16, 1),
+                pltpu.roll(value, LANES - 1, 1),
+                pltpu.roll(value, 1, 1),
+            )
+            for v, value in enumerate(values)
+        ]
+
+    def total(values):
+        while len(values) > 1:
+            values = [a + b for a, b in zip(values[::2], values[1::2])]
+        value = values[0]
+        for shift in (4, 2, 1):
+            value = value + pltpu.roll(value, shift, 0)
+        return jnp.sum(value, axis=1, keepdims=True)
+
+    source = [data[pl.ds(2 * v, 8, 2 * parts), :] for v in range(parts)]
+    conduct = [data[pl.ds(2 * v + 1, 8, 2 * parts), :] for v in range(parts)]
+    for v, near in enumerate(around(conduct)):
+        end = None
+        if v == 0:
+            end = jnp.logical_and(x == 0, row == 0)
+        if v == parts - 1:
+            end = jnp.logical_and(x == 1, row == 7)
+        diagonal = None
+        for slot, (edge, value) in enumerate(zip((None, end, z == 3, z == 0, y == 15, y == 0), near)):
+            if edge is not None:
+                value = jnp.where(edge, 0.0, value)
+            face = (0.5 * scale) * (conduct[v] + value)
+            diagonal = face if diagonal is None else diagonal + face
+            faces[slot, v] = face if edge is None else jnp.where(edge, 0.0, face)
+        faces[6, v] = diagonal
+
+    def operate(values):
+        return [
+            faces[6, v] * values[v] - sum(faces[slot, v] * value for slot, value in enumerate(near))
+            for v, near in enumerate(around(values))
+        ]
+
+    def products(values, images):
+        return total([a * a for a in values]), total([a * b for a, b in zip(values, images)])
+
+    first = operate(source)
+    norm, power = products(source, first)
+    alpha = norm / power
+    for v in range(parts):
+        answer[v] = alpha * source[v]
+        remain[v] = source[v] - alpha * first[v]
+        search[v] = source[v]
+        image[v] = first[v]
+
+    def advance(step, carry):
+        norm, alpha = carry
+        rest = [remain[v] for v in range(parts)]
+        images = operate(rest)
+        norm_next, power = products(rest, images)
+        beta = norm_next / norm
+        alpha = norm_next / (power - beta * norm_next / alpha)
+        for v in range(parts):
+            now = rest[v] + beta * search[v]
+            search[v] = now
+            out = images[v] + beta * image[v]
+            image[v] = out
+            answer[v] = answer[v] + alpha * now
+            remain[v] = rest[v] - alpha * out
+        return norm_next, alpha
+
+    lax.fori_loop(0, iters - 1, advance, (norm, alpha))
+
+
+def third_kernel(data, far_left, left, own, right, far_right, slab0, pressure, residual, answer, remain, search, image,
+                 faces, weights2, beside2, slab2, weights1, beside1, buf1, grow1, weights0, beside0, u0, grow0):
     wide, narrow = lax.axis_index("wide"), lax.axis_index("narrow")
     size = lax.axis_size("wide")
-    zeroed(answer)
-    coarsest(data, answer.at[pl.ds(8, data.shape[0] // 2)], remain, search, faces, ITERS)
-
     level = Level(2, 16, 8, weights2, beside2)
-    k, f = [(slab2.at[2 * a], slab2.at[2 * a + 1]) for a in range(2)]
-    zeroed(u2)
+    k, f, up2 = [(slab2.at[2 * a], slab2.at[2 * a + 1]) for a in range(3)]
+    zeroed(slab2)
+    for a in range(4):
+        slab2[a, 1:5] = far_left[a]
+        slab2[a, 11:15] = far_right[a]
+    place_two(slab2, left, 5)
+    place_two(slab2, right, 9)
+    place_two(slab2, own, 7)
+    level.setup(k, 1, 15, 2 * wide - 7, 2 * size)
+    level.start(up2, f, 1, 15)
+    level.half(1, up2, f, 2, 14)
+    level.half(0, up2, f, 2, 14)
+    level.half(1, up2, f, 3, 13)
+
+    coarsest(data, answer, remain, search, image, faces, ITERS)
     lane = lax.broadcasted_iota(jnp.int32, (8, LANES), 1)
     row = lax.broadcasted_iota(jnp.int32, (8, LANES), 0)
     where_from = (row // 2) * 16 + lane // 8
+    parts = answer.shape[0]
     for t in range(5):
-        line = answer[pl.ds(8 + wide - 2 + t, 1), :]
+        at = wide - 2 + t
+        inside = jnp.logical_and(at >= 0, at < size)
+        at = jnp.clip(at, 0, size - 1)
+        line = jnp.where(row == at // parts, answer[at % parts], 0.0)
+        line = jnp.where(inside, jnp.sum(line, axis=0, keepdims=True), 0.0)
         line = jnp.broadcast_to(line, (8, LANES))
         for half in range(2):
             i = 3 + 2 * t + half
-            u2[1, i] = slab2[5, i] + jnp.take_along_axis(line, where_from + 64 * half, axis=1)
-    up2 = (u2.at[0], u2.at[1])
-    level.setup(k, 3, 13, 2 * wide - 7, 2 * size)
+            slab2[5, i] = slab2[5, i] + jnp.take_along_axis(line, where_from + 64 * half, axis=1)
     level.half(0, up2, f, 3, 13)
     level.half(1, up2, f, 4, 12)
     level.half(0, up2, f, 4, 12)
@@ -300,9 +355,13 @@
     mid = Level(1, 12, 16, weights1, beside1)
     k1, f1, u1 = [(buf1.at[2 * a], buf1.at[2 * a + 1]) for a in range(3)]
     zeroed(u1[0])
-    for a in (0, 1, 2, 3, 5):
-        for place, part in enumerate((left1, own1, right1)):
-            buf1[a, 4 * place : 4 * place + 4] = part[a]
+    for slot, a in enumerate((0, 1, 2, 3, 5)):
+        for place, part in enumerate((left, own, right)):
+            for t in range(2):
+                both = part[4 * slot + 2 * t : 4 * slot + 2 * t + 2].reshape(16, LANES)
+                j = 4 * place + 2 * t
+                buf1[a, j] = jnp.where(mid.y_odd_lane, pltpu.roll(both, 1, 1), both)
+                buf1[a, j + 1] = jnp.where(mid.y_odd_lane, both, pltpu.roll(both, LANES - 1, 1))
     for j in range(12):
         i, side = 5 + j // 2, j % 2
         cell = jnp.where(level.odd, up2[1 - side][i], up2[side][i])
@@ -375,9 +434,9 @@
     block = jnp.concatenate([coefficient, rhs, packed], axis=0)
     whole = lax.all_gather(block, "narrow")
     left, right = shifted(whole, 1), shifted(whole, -1)
-    slab0, one, two = pl.pallas_call(
+    slab0, send = pl.pallas_call(
         first_kernel,
-        out_shape=(f32(6, 24, 32, LANES), f32(6, 4, 16, LANES), f32(4, 2, 8, LANES)),
+        out_shape=(f32(6, 24, 32, LANES), f32(32, 8, LANES)),
         scratch_shapes=[
             scratch(2, 7, 24, 32, LANES),
             scratch(24, 32, LANES),
@@ -386,33 +445,34 @@
             scratch(6, 12, 16, LANES),
             scratch(24, 32, LANES),
             scratch(24, 32, LANES),
-            scratch(8, 16, LANES),
+            scratch(12, 16, LANES),
         ],
         compiler_params=PARAMS,
         name="first",
     )(left, whole, right)
-    parts2 = [two if d == 0 else shifted(two, d) for d in (3, 2, 1, 0, -1, -2, -3)]
-    left1, right1 = shifted(one, 1), shifted(one, -1)
+    near = (shifted(send, 1), send, shifted(send, -1))
     count = lax.axis_size("wide")
-    slab2, out3 = pl.pallas_call(
+    out3, near_low, near_high = pl.pallas_call(
         second_kernel,
-        out_shape=(f32(6, 16, 8, LANES), f32(2 * count, LANES)),
-        scratch_shapes=[scratch(2, 7, 16, 8, LANES), scratch(16, 8, LANES)],
+        out_shape=(f32(2 * count, LANES), f32(4, 4, 8, LANES), f32(4, 4, 8, LANES)),
+        scratch_shapes=[scratch(6, 16, 8, LANES), scratch(2, 7, 16, 8, LANES), scratch(16, 8, LANES)],
         compiler_params=PARAMS,
         name="second",
-    )(*parts2)
+    )(*near)
+    far_left, far_right = shifted(near_high, 2), shifted(near_low, -2)
     data = lax.all_to_all(out3.reshape(count, 2, LANES), "wide", 0, 0).reshape(2 * count, LANES)
     return pl.pallas_call(
         third_kernel,
         out_shape=(f32(16, 8, LANES), f32(16, 8, LANES)),
         scratch_shapes=[
-            scratch(count + 16, LANES),
-            scratch(count, LANES),
-            scratch(count, LANES),
-            scratch(7, count, LANES),
+            scratch(count // 8, 8, LANES),
+            scratch(count // 8, 8, LANES),
+            scratch(count // 8, 8, LANES),
+            scratch(count // 8, 8, LANES),
+            scratch(7, count // 8, 8, LANES),
             scratch(2, 7, 16, 8, LANES),
             scratch(16, 8, LANES),
-            scratch(2, 16, 8, LANES),
+            scratch(6, 16, 8, LANES),
             scratch(2, 7, 12, 16, LANES),
             scratch(12, 16, LANES),
             scratch(6, 12, 16, LANES),
@@ -424,7 +484,7 @@
         ],
         compiler_params=PARAMS,
         name="third",
-    )(data, slab2, left1, one, right1, slab0)
+    )(data, far_left, *near, far_right, slab0)
 
 
 def solution(mesh):

time: 110 us -> 85.4 us (0.78)
  Pallas kernels: 28.1 us -> 13.6 us
  starting transfers between devices: 52.3 us -> 40.1 us
  waiting for transfers between devices: 15.6 us -> 17.6 us
    ppermute x10 -> x6, starting transfers between devices: 35.2 us -> 23.3 us  [shifted(): return lax.ppermute(block, 'wide', pairs)]
    pallas_call x1, Pallas kernels: 16.6 us -> 8.46 us  [local(): pl.pallas_call(third_kernel, out_shape=(f32(16, 8, LANES), f32(16, 8, LAN...]
    pallas_call x2, Pallas kernels: 11.5 us -> 5.17 us  [the longest x1 3.98 us: local(): pl.pallas_call(first_kernel, out_shape=(f32(6, 24, 32, LANES), f32(32, 8,...]
    ppermute x10 -> x6, waiting for transfers between devices: 11.1 us -> 13.4 us  [shifted(): return lax.ppermute(block, 'wide', pairs)]
  transfers between devices with their start and end apart: 11 -> 7, of which waited for: 6 -> 7; matrix products, arithmetic and copies ran while one was open for 0% -> 0% of each run, Pallas kernels for 0% -> 0%
where the time goes in v2:
time: 85.4 us; the launch traced here: 84.9 us
  starting transfers between devices  40.1 us (47%)
  waiting for transfers between devices  17.6 us (21%)
  Pallas kernels  13.6 us (16%)
  blocking collectives  11.3 us (13%)
  other arithmetic  1.67 us (2%)
    ppermute x6, starting transfers between devices, shifted(): return lax.ppermute(block, 'wide', pairs)  23.3 us
    all_to_all x1, starting transfers between devices, local(): lax.all_to_all(out3.reshape(count, 2, LANES), 'wide', 0, 0)  16.8 us
    ppermute x6, waiting for transfers between devices, shifted(): return lax.ppermute(block, 'wide', pairs)  13.4 us
    all_gather x1, blocking collectives, local(): whole = lax.all_gather(block, 'narrow')  11.3 us
    pallas_call x1, Pallas kernels, local(): pl.pallas_call(third_kernel, out_shape=(f32(16, 8, LANES), f32(16, 8, LAN...  8.46 us
    all_to_all x1, waiting for transfers between devices, local(): lax.all_to_all(out3.reshape(count, 2, LANES), 'wide', 0, 0)  4.12 us
    pallas_call x1, Pallas kernels, local(): pl.pallas_call(first_kernel, out_shape=(f32(6, 24, 32, LANES), f32(32, 8,...  3.98 us
  transfers between devices with their start and end apart: 7, of which 7 were waited for; matrix products, arithmetic and copies ran while one was open for 0% of the time, Pallas kernels for 0%

profile of v2, /device:TPU:1, one launch (start us, length us, event | category | flops | bytes accessed | tf_op | source)
XLA Modules:
  0.0 84.9 jit_solution(9240167240040411075)
XLA Ops:
  0.6 0.8 slice_select_fusion
  1.4 0.9 %pad_maximum_fusion = f32[40,8,128]{2,1,0:T(8,128)S(1)} fusion(f32[8,8,128]{2,1,0:T(8,128)S(1)} %slice_select_fusion, f32[16,8,128]{2,1,0:T(8,128)} %param.3, f32[16,8,128]{2,1,0:T(8,128)} %param.4), kind=kLoop, calls=%fused_computation | loop fusion | flops 81920 | bytes 327680 | tf_op jit(solution)/shard_map/concatenate | solution.py:434
  2.3 11.3 %all-gather = f32[160,8,128]{2,1,0:T(8,128)S(1)} all-gather(f32[40,8,128]{2,1,0:T(8,128)S(1)} %pad_maximum_fusion), channel_id=2, replica_groups=mesh['wide'=128,'narrow'=4] {'narrow'}, dimensions={0}, use_global_device_ids=true | all-gather | bytes 819200 | tf_op jit(solution)/shard_map/all_gather | solution.py:435
  13.6 10.5 %collective-permute-start.1 = (f32[4,40,8,128]{3,2,1,0:T(8,128)S(1)}, f32[4,40,8,128]{3,2,1,0:T(8,128)S(1)}, u32[]{:S(2)}, u32[]{:S(2)}) collective-permute-start(f32[4,40,8,128]{3,2,1,0:T(8,128)S(1)} %bitcast.3), channel_id=1, source_target_pairs={{4,0},{8,4},{12,8},{16,12},{20,16},{24,20},{28,24},{32,28},{36,32}... | collective-permute-start | bytes 1966088 | tf_op jit(solution)/shard_map/ppermute | solution.py:427
  24.1 1.9 %collective-permute-start = (f32[4,40,8,128]{3,2,1,0:T(8,128)S(1)}, f32[4,40,8,128]{3,2,1,0:T(8,128)S(1)}, u32[]{:S(2)}, u32[]{:S(2)}) collective-permute-start(f32[4,40,8,128]{3,2,1,0:T(8,128)S(1)} %bitcast.4), channel_id=1, source_target_pairs={{0,4},{4,8},{8,12},{12,16},{16,20},{20,24},{24,28},{28,32},{32,36}... | collective-permute-start | bytes 1966088 | tf_op jit(solution)/shard_map/ppermute | solution.py:427
  26.1 2.5 %collective-permute-done.1.right = f32[4,40,8,128]{3,2,1,0:T(8,128)S(1)} collective-permute-done((f32[4,40,8,128]{3,2,1,0:T(8,128)S(1)}, f32[4,40,8,128]{3,2,1,0:T(8,128)S(1)}, u32[]{:S(2)}, u32[]{:S(2)}) %collective-permute-start.1) | collective-permute-done | bytes 655392 | tf_op jit(solution)/shard_map/ppermute | solution.py:427
  28.5 5.0 %collective-permute-done.left = f32[4,40,8,128]{3,2,1,0:T(8,128)S(1)} collective-permute-done((f32[4,40,8,128]{3,2,1,0:T(8,128)S(1)}, f32[4,40,8,128]{3,2,1,0:T(8,128)S(1)}, u32[]{:S(2)}, u32[]{:S(2)}) %collective-permute-start) | collective-permute-done | bytes 655392 | tf_op jit(solution)/shard_map/ppermute | solution.py:427
  33.6 4.0 %first.1 = (f32[6,24,32,128]{3,2,1,0:T(8,128)S(1)}, f32[32,8,128]{2,1,0:T(8,128)S(1)}) custom-call(f32[4,40,8,128]{3,2,1,0:T(8,128)S(1)} %collective-permute-done.left, f32[4,40,8,128]{3,2,1,0:T(8,128)S(1)} %bitcast.5, f32[4,40,8,128]{3,2,1,0:T(8,128)S(1)} %collective-permute-done.1.right), custom_call_target="tpu_custom_call" | custom-call | tf_op jit(solution)/shard_map/first/pallas_call | solution.py:437
  37.6 1.9 %collective-permute-start.3 = (f32[32,8,128]{2,1,0:T(8,128)S(1)}, f32[32,8,128]{2,1,0:T(8,128)S(1)}, u32[]{:S(2)}, u32[]{:S(2)}) collective-permute-start(f32[32,8,128]{2,1,0:T(8,128)S(1)} %get-tuple-element.7.own), channel_id=1, source_target_pairs={{4,0},{8,4},{12,8},{16,12},{20,16},{24,20},{28,24},{32,28},{36,32}... | collective-permute-start | bytes 393224 | tf_op jit(solution)/shard_map/ppermute | solution.py:427
  39.5 4.4 %collective-permute-start.2 = (f32[32,8,128]{2,1,0:T(8,128)S(1)}, f32[32,8,128]{2,1,0:T(8,128)S(1)}, u32[]{:S(2)}, u32[]{:S(2)}) collective-permute-start(f32[32,8,128]{2,1,0:T(8,128)S(1)} %get-tuple-element.7.own), channel_id=1, source_target_pairs={{0,4},{4,8},{8,12},{12,16},{16,20},{20,24},{24,28},{28,32},{32,36}... | collective-permute-start | bytes 393224 | tf_op jit(solution)/shard_map/ppermute | solution.py:427
  43.9 0.7 collective-permute-done.3.right
  44.6 1.2 %collective-permute-done.2.left = f32[32,8,128]{2,1,0:T(8,128)S(1)} collective-permute-done((f32[32,8,128]{2,1,0:T(8,128)S(1)}, f32[32,8,128]{2,1,0:T(8,128)S(1)}, u32[]{:S(2)}, u32[]{:S(2)}) %collective-permute-start.2) | collective-permute-done | bytes 131104 | tf_op jit(solution)/shard_map/ppermute | solution.py:427
  45.8 1.2 %second.1 = (f32[256,128]{1,0:T(8,128)}, f32[4,4,8,128]{3,2,1,0:T(8,128)S(1)}, f32[4,4,8,128]{3,2,1,0:T(8,128)S(1)}) custom-call(f32[32,8,128]{2,1,0:T(8,128)S(1)} %collective-permute-done.2.left, f32[32,8,128]{2,1,0:T(8,128)S(1)} %get-tuple-element.7.own, f32[32,8,128]{2,1,0:T(8,128)S(1)} %collective-permute-done.3.right), custom_call_target="tpu_custom_call" | custom-call | tf_op jit(solution)/shard_map/second/pallas_call | solution.py:455
  47.0 16.8 %all-to-all-start = ((f32[128,2,128]{2,1,0:T(2,128)}), f32[128,2,128]{2,1,0:T(2,128)S(1)}, u32[]{:S(2)}, u32[]{:S(2)}) async-start(f32[128,2,128]{2,1,0:T(2,128)} %bitcast.1), calls=%async_computation | async-start | bytes 262144 | tf_op jit(solution)/shard_map/all_to_all | solution.py:463
  63.8 3.3 %collective-permute-start.4 = (f32[4,4,8,128]{3,2,1,0:T(8,128)S(1)}, f32[4,4,8,128]{3,2,1,0:T(8,128)S(1)}, u32[]{:S(2)}, u32[]{:S(2)}) collective-permute-start(f32[4,4,8,128]{3,2,1,0:T(8,128)S(1)} %get-tuple-element.9), channel_id=1, source_target_pairs={{0,8},{4,12},{8,16},{12,20},{16,24},{20,28},{24,32},{28,36},{32,40... | collective-permute-start | bytes 196616 | tf_op jit(solution)/shard_map/ppermute | solution.py:427
  67.1 1.3 %collective-permute-start.5 = (f32[4,4,8,128]{3,2,1,0:T(8,128)S(1)}, f32[4,4,8,128]{3,2,1,0:T(8,128)S(1)}, u32[]{:S(2)}, u32[]{:S(2)}) collective-permute-start(f32[4,4,8,128]{3,2,1,0:T(8,128)S(1)} %get-tuple-element.10), channel_id=1, source_target_pairs={{8,0},{12,4},{16,8},{20,12},{24,16},{28,20},{32,24},{36,28},{40,32... | collective-permute-start | bytes 196616 | tf_op jit(solution)/shard_map/ppermute | solution.py:427
  68.4 0.4 collective-permute-done.4.far_left
  68.8 3.6 %collective-permute-done.5.far_right = f32[4,4,8,128]{3,2,1,0:T(8,128)S(1)} collective-permute-done((f32[4,4,8,128]{3,2,1,0:T(8,128)S(1)}, f32[4,4,8,128]{3,2,1,0:T(8,128)S(1)}, u32[]{:S(2)}, u32[]{:S(2)}) %collective-permute-start.5) | collective-permute-done | bytes 65568 | tf_op jit(solution)/shard_map/ppermute | solution.py:427
  72.4 4.1 %all-to-all-done = f32[128,2,128]{2,1,0:T(2,128)S(1)} async-done(((f32[128,2,128]{2,1,0:T(2,128)}), f32[128,2,128]{2,1,0:T(2,128)S(1)}, u32[]{:S(2)}, u32[]{:S(2)}) %all-to-all-start) | async-done | bytes 131104 | tf_op jit(solution)/shard_map/all_to_all | solution.py:463
  76.5 8.5 %third.1 = (f32[16,8,128]{2,1,0:T(8,128)}, f32[16,8,128]{2,1,0:T(8,128)}) custom-call(f32[256,128]{1,0:T(8,128)S(1)} %bitcast.6, f32[4,4,8,128]{3,2,1,0:T(8,128)S(1)} %collective-permute-done.4.far_left, f32[32,8,128]{2,1,0:T(8,128)S(1)} %collective-permute-done.2.left, f32[32,8,128]{2,1,0:T(8,128)S(1)} %get-tuple-element.7.own, ...), custom_call_target="tpu_custom_call" | custom-call | tf_op jit(solution)/shard_map/third/pallas_call | solution.py:464
Async XLA Ops:
  13.6 14.9 %collective-permute-start.1 = (f32[4,40,8,128]{3,2,1,0:T(8,128)S(1)}, f32[4,40,8,128]{3,2,1,0:T(8,128)S(1)}, u32[]{:S(2)}, u32[]{:S(2)}) collective-permute-start(f32[4,40,8,128]{3,2,1,0:T(8,128)S(1)} %bitcast.3), channel_id=1, source_target_pairs={{4,0},{8,4},{12,8},{16,12},{20,16},{24,20},{28,24},{32,28},{36,32}... | collective-permute-start | bytes 1966088 | tf_op jit(solution)/shard_map/ppermute | solution.py:427
  24.1 9.4 %collective-permute-start = (f32[4,40,8,128]{3,2,1,0:T(8,128)S(1)}, f32[4,40,8,128]{3,2,1,0:T(8,128)S(1)}, u32[]{:S(2)}, u32[]{:S(2)}) collective-permute-start(f32[4,40,8,128]{3,2,1,0:T(8,128)S(1)} %bitcast.4), channel_id=1, source_target_pairs={{0,4},{4,8},{8,12},{12,16},{16,20},{20,24},{24,28},{28,32},{32,36}... | collective-permute-start | bytes 1966088 | tf_op jit(solution)/shard_map/ppermute | solution.py:427
  37.6 7.0 %collective-permute-start.3 = (f32[32,8,128]{2,1,0:T(8,128)S(1)}, f32[32,8,128]{2,1,0:T(8,128)S(1)}, u32[]{:S(2)}, u32[]{:S(2)}) collective-permute-start(f32[32,8,128]{2,1,0:T(8,128)S(1)} %get-tuple-element.7.own), channel_id=1, source_target_pairs={{4,0},{8,4},{12,8},{16,12},{20,16},{24,20},{28,24},{32,28},{36,32}... | collective-permute-start | bytes 393224 | tf_op jit(solution)/shard_map/ppermute | solution.py:427
  39.5 6.3 %collective-permute-start.2 = (f32[32,8,128]{2,1,0:T(8,128)S(1)}, f32[32,8,128]{2,1,0:T(8,128)S(1)}, u32[]{:S(2)}, u32[]{:S(2)}) collective-permute-start(f32[32,8,128]{2,1,0:T(8,128)S(1)} %get-tuple-element.7.own), channel_id=1, source_target_pairs={{0,4},{4,8},{8,12},{12,16},{16,20},{20,24},{24,28},{28,32},{32,36}... | collective-permute-start | bytes 393224 | tf_op jit(solution)/shard_map/ppermute | solution.py:427
  47.0 29.5 %all-to-all-start = ((f32[128,2,128]{2,1,0:T(2,128)}), f32[128,2,128]{2,1,0:T(2,128)S(1)}, u32[]{:S(2)}, u32[]{:S(2)}) async-start(f32[128,2,128]{2,1,0:T(2,128)} %bitcast.1), calls=%async_computation | async-start | bytes 262144 | tf_op jit(solution)/shard_map/all_to_all | solution.py:463
  63.8 5.0 %collective-permute-start.4 = (f32[4,4,8,128]{3,2,1,0:T(8,128)S(1)}, f32[4,4,8,128]{3,2,1,0:T(8,128)S(1)}, u32[]{:S(2)}, u32[]{:S(2)}) collective-permute-start(f32[4,4,8,128]{3,2,1,0:T(8,128)S(1)} %get-tuple-element.9), channel_id=1, source_target_pairs={{0,8},{4,12},{8,16},{12,20},{16,24},{20,28},{24,32},{28,36},{32,40... | collective-permute-start | bytes 196616 | tf_op jit(solution)/shard_map/ppermute | solution.py:427
  67.1 5.3 %collective-permute-start.5 = (f32[4,4,8,128]{3,2,1,0:T(8,128)S(1)}, f32[4,4,8,128]{3,2,1,0:T(8,128)S(1)}, u32[]{:S(2)}, u32[]{:S(2)}) collective-permute-start(f32[4,4,8,128]{3,2,1,0:T(8,128)S(1)} %get-tuple-element.10), channel_id=1, source_target_pairs={{8,0},{12,4},{16,8},{20,12},{24,16},{28,20},{32,24},{36,28},{40,32... | collective-permute-start | bytes 196616 | tf_op jit(solution)/shard_map/ppermute | solution.py:427

commit v3 on v2

--- a/solution.py
+++ b/solution.py
@@ -109,24 +109,42 @@
         ref[...] = jnp.zeros(ref.shape, ref.dtype)
 
 
-def first_kernel(left, own, right, slab, send, weights0, beside0, weights1, beside1, buf1, sums, sums1, tmp):
+def spread_kernel(whole, to_right, to_left):
+    for n in range(4):
+        to_right[n, 0:13] = whole[n, 3:16]
+        to_right[n, 13:25] = whole[n, 20:32]
+        to_right[n, 25:32] = whole[n, 33:40]
+        to_left[n, 0:13] = whole[n, 0:13]
+        to_left[n, 13:25] = whole[n, 16:28]
+        to_left[n, 25:32] = whole[n, 32:39]
+
+
+def first_kernel(right, own, left, slab, send, weights0, beside0, weights1, beside1, buf1, sums, sums1, tmp):
     wide = lax.axis_index("wide")
     k0, f0, u0 = [(slab.at[2 * a], slab.at[2 * a + 1]) for a in range(3)]
     fine = Level(0, 24, 32, weights0, beside0)
     zeroed(u0[0])
     odd8 = fine.odd[:8]
-    for base, part in ((0, left), (8, own), (16, right)):
-        for n in range(4):
-            z = slice(8 * n, 8 * n + 8)
-
-            def unpack(i, part=part, n=n, z=z, base=base):
-                for group, target in ((0, k0), (16, f0)):
-                    even, uneven = part[n, group + 2 * i], part[n, group + 2 * i + 1]
-                    target[0][base + i, z] = jnp.where(odd8, uneven, even)
-                    target[1][base + i, z] = jnp.where(odd8, even, uneven)
-                u0[1][base + i, z] = part[n, 32 + i]
-
-            loop(0, 8, unpack)
+
+    def row(base, n, kind, x):
+        first, count = {"k": (0, 16), "f": (16, 16), "g": (32, 8)}[kind]
+        start, kept = {"k": (0, 13), "f": (13, 12), "g": (25, 7)}[kind]
+        if base == 8:
+            return own[n, first + x]
+        x = x - (count - kept) if base == 0 else x
+        if x < 0 or x >= kept:
+            return jnp.zeros((8, LANES), jnp.float32)
+        return (left if base == 0 else right)[n, start + x]
+
+    for n in range(4):
+        z = slice(8 * n, 8 * n + 8)
+        for i in range(1, 23):
+            base, x = i // 8 * 8, 2 * (i % 8)
+            for kind, target in (("k", k0), ("f", f0)):
+                even, uneven = row(base, n, kind, x), row(base, n, kind, x + 1)
+                target[0][i, z] = jnp.where(odd8, uneven, even)
+                target[1][i, z] = jnp.where(odd8, even, uneven)
+            u0[1][i, z] = row(base, n, "g", i % 8)
     fine.setup(k0, 2, 22, 8 * wide - 8, 8 * lax.axis_size("wide"))
     fine.half(0, u0, f0, 2, 22)
     fine.half(1, u0, f0, 2, 22)
@@ -228,7 +246,8 @@
         out[8 * w : 8 * w + 8] = both
 
 
-def coarsest(data, answer, remain, search, image, faces, iters):
+def coarsest(data, answer, vectors, faces, iters):
+    remain, search, image = (vectors.at[a] for a in range(3))
     parts = data.shape[0] // 16
     scale = 0.25**3
     row = lax.broadcasted_iota(jnp.int32, (8, LANES), 0)
@@ -285,36 +304,34 @@
     def products(values, images):
         return total([a * a for a in values]), total([a * b for a, b in zip(values, images)])
 
-    first = operate(source)
-    norm, power = products(source, first)
-    alpha = norm / power
-    for v in range(parts):
-        answer[v] = alpha * source[v]
-        remain[v] = source[v] - alpha * first[v]
-        search[v] = source[v]
-        image[v] = first[v]
-
     def advance(step, carry):
-        norm, alpha = carry
         rest = [remain[v] for v in range(parts)]
         images = operate(rest)
-        norm_next, power = products(rest, images)
-        beta = norm_next / norm
-        alpha = norm_next / (power - beta * norm_next / alpha)
+        norm = total([a * a for a in rest])
+        power = total([a * b for a, b in zip(rest, images)])
+        if carry is None:
+            for v in range(parts):
+                answer[v] = jnp.zeros_like(rest[v])
+        else:
+            beta = norm * carry[0]
+            power = power - beta * beta * carry[1]
+        alpha = norm / power
         for v in range(parts):
-            now = rest[v] + beta * search[v]
-            search[v] = now
-            out = images[v] + beta * image[v]
-            image[v] = out
+            now, one = rest[v], images[v]
+            if carry is not None:
+                now, one = now + beta * search[v], one + beta * image[v]
+            search[v], image[v] = now, one
             answer[v] = answer[v] + alpha * now
-            remain[v] = rest[v] - alpha * out
-        return norm_next, alpha
-
-    lax.fori_loop(0, iters - 1, advance, (norm, alpha))
-
-
-def third_kernel(data, far_left, left, own, right, far_right, slab0, pressure, residual, answer, remain, search, image,
-                 faces, weights2, beside2, slab2, weights1, beside1, buf1, grow1, weights0, beside0, u0, grow0):
+            remain[v] = rest[v] - alpha * one
+        return 1.0 / norm, power
+
+    for v, value in enumerate(source):
+        remain[v] = value
+    lax.fori_loop(0, iters - 1, advance, advance(0, None))
+
+
+def third_kernel(data, far_left, left, own, right, far_right, slab0, pressure, residual, answer, vectors, faces,
+                 weights2, beside2, slab2, weights1, beside1, buf1, grow1, weights0, beside0, u0, grow0):
     wide, narrow = lax.axis_index("wide"), lax.axis_index("narrow")
     size = lax.axis_size("wide")
     level = Level(2, 16, 8, weights2, beside2)
@@ -332,7 +349,7 @@
     level.half(0, up2, f, 2, 14)
     level.half(1, up2, f, 3, 13)
 
-    coarsest(data, answer, remain, search, image, faces, ITERS)
+    coarsest(data, answer, vectors, faces, ITERS)
     lane = lax.broadcasted_iota(jnp.int32, (8, LANES), 1)
     row = lax.broadcasted_iota(jnp.int32, (8, LANES), 0)
     where_from = (row // 2) * 16 + lane // 8
@@ -431,9 +448,15 @@
     shape = (8, 8, LANES)
     odd = (lax.broadcasted_iota(jnp.int32, shape, 1) + lax.broadcasted_iota(jnp.int32, shape, 2)) % 2 == 1
     packed = jnp.where(odd, guess[0::2], guess[1::2])
-    block = jnp.concatenate([coefficient, rhs, packed], axis=0)
-    whole = lax.all_gather(block, "narrow")
-    left, right = shifted(whole, 1), shifted(whole, -1)
+    whole = lax.all_gather(jnp.concatenate([coefficient, rhs, packed], axis=0), "narrow")
+    to_right, to_left = pl.pallas_call(
+        spread_kernel,
+        out_shape=(f32(4, 32, 8, LANES), f32(4, 32, 8, LANES)),
+        compiler_params=PARAMS,
+        name="spread",
+    )(whole)
+    right = shifted(to_left, -1)
+    left = shifted(to_right, 1)
     slab0, send = pl.pallas_call(
         first_kernel,
         out_shape=(f32(6, 24, 32, LANES), f32(32, 8, LANES)),
@@ -449,7 +472,7 @@
         ],
         compiler_params=PARAMS,
         name="first",
-    )(left, whole, right)
+    )(right, whole, left)
     near = (shifted(send, 1), send, shifted(send, -1))
     count = lax.axis_size("wide")
     out3, near_low, near_high = pl.pallas_call(
@@ -466,9 +489,7 @@
         out_shape=(f32(16, 8, LANES), f32(16, 8, LANES)),
         scratch_shapes=[
             scratch(count // 8, 8, LANES),
-            scratch(count // 8, 8, LANES),
-            scratch(count // 8, 8, LANES),
-            scratch(count // 8, 8, LANES),
+            scratch(3, count // 8, 8, LANES),
             scratch(7, count // 8, 8, LANES),
             scratch(2, 7, 16, 8, LANES),
             scratch(16, 8, LANES),

time: 85.4 us -> 84 us (0.984)
  waiting for transfers between devices: 17.6 us -> 16.2 us
    ppermute x6, waiting for transfers between devices: 13.4 us -> 12 us  [shifted(): return lax.ppermute(block, 'wide', pairs)]
where the time goes in v3:
time: 84 us; the launch traced here: 83.6 us
  starting transfers between devices  40.1 us (48%)
  waiting for transfers between devices  16.2 us (19%)
  Pallas kernels  13.7 us (16%)
  blocking collectives  11.3 us (13%)
  other arithmetic  1.67 us (2%)
    ppermute x6, starting transfers between devices, shifted(): return lax.ppermute(block, 'wide', pairs)  23.3 us
    all_to_all x1, starting transfers between devices, local(): lax.all_to_all(out3.reshape(count, 2, LANES), 'wide', 0, 0)  16.8 us
    ppermute x6, waiting for transfers between devices, shifted(): return lax.ppermute(block, 'wide', pairs)  12 us
    all_gather x1, blocking collectives, local(): lax.all_gather(jnp.concatenate([coefficient, rhs, packed], axis=0), 'narr...  11.3 us
    pallas_call x1, Pallas kernels, local(): pl.pallas_call(third_kernel, out_shape=(f32(16, 8, LANES), f32(16, 8, LAN...  8.46 us
    all_to_all x1, waiting for transfers between devices, local(): lax.all_to_all(out3.reshape(count, 2, LANES), 'wide', 0, 0)  4.12 us
    pallas_call x1, Pallas kernels, local(): pl.pallas_call(first_kernel, out_shape=(f32(6, 24, 32, LANES), f32(32, 8,...  3.98 us
  transfers between devices with their start and end apart: 7, of which 7 were waited for; matrix products, arithmetic and copies ran while one was open for 0% of the time, Pallas kernels for 0%

profile of v3, /device:TPU:1, one launch (start us, length us, event | category | flops | bytes accessed | tf_op | source)
XLA Modules:
  0.0 83.6 jit_solution(4551189450998531826)
XLA Ops:
  0.6 0.8 slice_select_fusion
  1.4 0.9 %pad_maximum_fusion = f32[40,8,128]{2,1,0:T(8,128)S(1)} fusion(f32[8,8,128]{2,1,0:T(8,128)S(1)} %slice_select_fusion, f32[16,8,128]{2,1,0:T(8,128)} %param.3, f32[16,8,128]{2,1,0:T(8,128)} %param.4), kind=kLoop, calls=%fused_computation | loop fusion | flops 81920 | bytes 327680 | tf_op jit(solution)/shard_map/concatenate | solution.py:451
  2.3 11.3 %all-gather = f32[160,8,128]{2,1,0:T(8,128)S(1)} all-gather(f32[40,8,128]{2,1,0:T(8,128)S(1)} %pad_maximum_fusion), channel_id=2, replica_groups=mesh['wide'=128,'narrow'=4] {'narrow'}, dimensions={0}, use_global_device_ids=true | all-gather | bytes 819200 | tf_op jit(solution)/shard_map/all_gather | solution.py:451
  13.6 0.1 spread.1
  13.7 10.5 %collective-permute-start = (f32[4,32,8,128]{3,2,1,0:T(8,128)S(1)}, f32[4,32,8,128]{3,2,1,0:T(8,128)S(1)}, u32[]{:S(2)}, u32[]{:S(2)}) collective-permute-start(f32[4,32,8,128]{3,2,1,0:T(8,128)S(1)} %get-tuple-element.9), channel_id=1, source_target_pairs={{4,0},{8,4},{12,8},{16,12},{20,16},{24,20},{28,24},{32,28},{36,32}... | collective-permute-start | bytes 1572872 | tf_op jit(solution)/shard_map/ppermute | solution.py:444
  24.2 1.9 %collective-permute-start.1 = (f32[4,32,8,128]{3,2,1,0:T(8,128)S(1)}, f32[4,32,8,128]{3,2,1,0:T(8,128)S(1)}, u32[]{:S(2)}, u32[]{:S(2)}) collective-permute-start(f32[4,32,8,128]{3,2,1,0:T(8,128)S(1)} %get-tuple-element.10), channel_id=1, source_target_pairs={{0,4},{4,8},{8,12},{12,16},{16,20},{20,24},{24,28},{28,32},{32,36}... | collective-permute-start | bytes 1572872 | tf_op jit(solution)/shard_map/ppermute | solution.py:444
  26.1 1.1 %collective-permute-done.right = f32[4,32,8,128]{3,2,1,0:T(8,128)S(1)} collective-permute-done((f32[4,32,8,128]{3,2,1,0:T(8,128)S(1)}, f32[4,32,8,128]{3,2,1,0:T(8,128)S(1)}, u32[]{:S(2)}, u32[]{:S(2)}) %collective-permute-start) | collective-permute-done | bytes 524320 | tf_op jit(solution)/shard_map/ppermute | solution.py:444
  27.2 5.0 %collective-permute-done.1.left = f32[4,32,8,128]{3,2,1,0:T(8,128)S(1)} collective-permute-done((f32[4,32,8,128]{3,2,1,0:T(8,128)S(1)}, f32[4,32,8,128]{3,2,1,0:T(8,128)S(1)}, u32[]{:S(2)}, u32[]{:S(2)}) %collective-permute-start.1) | collective-permute-done | bytes 524320 | tf_op jit(solution)/shard_map/ppermute | solution.py:444
  32.2 4.0 %first.1 = (f32[6,24,32,128]{3,2,1,0:T(8,128)S(1)}, f32[32,8,128]{2,1,0:T(8,128)S(1)}) custom-call(f32[4,32,8,128]{3,2,1,0:T(8,128)S(1)} %collective-permute-done.right, f32[4,40,8,128]{3,2,1,0:T(8,128)S(1)} %bitcast.4, f32[4,32,8,128]{3,2,1,0:T(8,128)S(1)} %collective-permute-done.1.left), custom_call_target="tpu_custom_call" | custom-call | tf_op jit(solution)/shard_map/first/pallas_call | solution.py:460
  36.2 1.9 %collective-permute-start.3 = (f32[32,8,128]{2,1,0:T(8,128)S(1)}, f32[32,8,128]{2,1,0:T(8,128)S(1)}, u32[]{:S(2)}, u32[]{:S(2)}) collective-permute-start(f32[32,8,128]{2,1,0:T(8,128)S(1)} %get-tuple-element.11.own), channel_id=1, source_target_pairs={{4,0},{8,4},{12,8},{16,12},{20,16},{24,20},{28,24},{32,28},{36,32}... | collective-permute-start | bytes 393224 | tf_op jit(solution)/shard_map/ppermute | solution.py:444
  38.2 4.4 %collective-permute-start.2 = (f32[32,8,128]{2,1,0:T(8,128)S(1)}, f32[32,8,128]{2,1,0:T(8,128)S(1)}, u32[]{:S(2)}, u32[]{:S(2)}) collective-permute-start(f32[32,8,128]{2,1,0:T(8,128)S(1)} %get-tuple-element.11.own), channel_id=1, source_target_pairs={{0,4},{4,8},{8,12},{12,16},{16,20},{20,24},{24,28},{28,32},{32,36}... | collective-permute-start | bytes 393224 | tf_op jit(solution)/shard_map/ppermute | solution.py:444
  42.6 0.7 collective-permute-done.3.right
  43.3 1.2 %collective-permute-done.2.left = f32[32,8,128]{2,1,0:T(8,128)S(1)} collective-permute-done((f32[32,8,128]{2,1,0:T(8,128)S(1)}, f32[32,8,128]{2,1,0:T(8,128)S(1)}, u32[]{:S(2)}, u32[]{:S(2)}) %collective-permute-start.2) | collective-permute-done | bytes 131104 | tf_op jit(solution)/shard_map/ppermute | solution.py:444
  44.5 1.2 %second.1 = (f32[256,128]{1,0:T(8,128)}, f32[4,4,8,128]{3,2,1,0:T(8,128)S(1)}, f32[4,4,8,128]{3,2,1,0:T(8,128)S(1)}) custom-call(f32[32,8,128]{2,1,0:T(8,128)S(1)} %collective-permute-done.2.left, f32[32,8,128]{2,1,0:T(8,128)S(1)} %get-tuple-element.11.own, f32[32,8,128]{2,1,0:T(8,128)S(1)} %collective-permute-done.3.right), custom_call_target="tpu_custom_call" | custom-call | tf_op jit(solution)/shard_map/second/pallas_call | solution.py:478
  45.7 16.8 %all-to-all-start = ((f32[128,2,128]{2,1,0:T(2,128)}), f32[128,2,128]{2,1,0:T(2,128)S(1)}, u32[]{:S(2)}, u32[]{:S(2)}) async-start(f32[128,2,128]{2,1,0:T(2,128)} %bitcast.1), calls=%async_computation | async-start | bytes 262144 | tf_op jit(solution)/shard_map/all_to_all | solution.py:486
  62.4 3.3 %collective-permute-start.4 = (f32[4,4,8,128]{3,2,1,0:T(8,128)S(1)}, f32[4,4,8,128]{3,2,1,0:T(8,128)S(1)}, u32[]{:S(2)}, u32[]{:S(2)}) collective-permute-start(f32[4,4,8,128]{3,2,1,0:T(8,128)S(1)} %get-tuple-element.13), channel_id=1, source_target_pairs={{0,8},{4,12},{8,16},{12,20},{16,24},{20,28},{24,32},{28,36},{32,40... | collective-permute-start | bytes 196616 | tf_op jit(solution)/shard_map/ppermute | solution.py:444
  65.7 1.3 %collective-permute-start.5 = (f32[4,4,8,128]{3,2,1,0:T(8,128)S(1)}, f32[4,4,8,128]{3,2,1,0:T(8,128)S(1)}, u32[]{:S(2)}, u32[]{:S(2)}) collective-permute-start(f32[4,4,8,128]{3,2,1,0:T(8,128)S(1)} %get-tuple-element.14), channel_id=1, source_target_pairs={{8,0},{12,4},{16,8},{20,12},{24,16},{28,20},{32,24},{36,28},{40,32... | collective-permute-start | bytes 196616 | tf_op jit(solution)/shard_map/ppermute | solution.py:444
  67.0 0.4 collective-permute-done.4.far_left
  67.4 3.6 %collective-permute-done.5.far_right = f32[4,4,8,128]{3,2,1,0:T(8,128)S(1)} collective-permute-done((f32[4,4,8,128]{3,2,1,0:T(8,128)S(1)}, f32[4,4,8,128]{3,2,1,0:T(8,128)S(1)}, u32[]{:S(2)}, u32[]{:S(2)}) %collective-permute-start.5) | collective-permute-done | bytes 65568 | tf_op jit(solution)/shard_map/ppermute | solution.py:444
  71.0 4.1 %all-to-all-done = f32[128,2,128]{2,1,0:T(2,128)S(1)} async-done(((f32[128,2,128]{2,1,0:T(2,128)}), f32[128,2,128]{2,1,0:T(2,128)S(1)}, u32[]{:S(2)}, u32[]{:S(2)}) %all-to-all-start) | async-done | bytes 131104 | tf_op jit(solution)/shard_map/all_to_all | solution.py:486
  75.2 8.5 %third.1 = (f32[16,8,128]{2,1,0:T(8,128)}, f32[16,8,128]{2,1,0:T(8,128)}) custom-call(f32[256,128]{1,0:T(8,128)S(1)} %bitcast.5, f32[4,4,8,128]{3,2,1,0:T(8,128)S(1)} %collective-permute-done.4.far_left, f32[32,8,128]{2,1,0:T(8,128)S(1)} %collective-permute-done.2.left, f32[32,8,128]{2,1,0:T(8,128)S(1)} %get-tuple-element.11.own, ...), custom_call_target="tpu_custom_call" | custom-call | tf_op jit(solution)/shard_map/third/pallas_call | solution.py:487
Async XLA Ops:
  13.7 13.5 %collective-permute-start = (f32[4,32,8,128]{3,2,1,0:T(8,128)S(1)}, f32[4,32,8,128]{3,2,1,0:T(8,128)S(1)}, u32[]{:S(2)}, u32[]{:S(2)}) collective-permute-start(f32[4,32,8,128]{3,2,1,0:T(8,128)S(1)} %get-tuple-element.9), channel_id=1, source_target_pairs={{4,0},{8,4},{12,8},{16,12},{20,16},{24,20},{28,24},{32,28},{36,32}... | collective-permute-start | bytes 1572872 | tf_op jit(solution)/shard_map/ppermute | solution.py:444
  24.2 8.0 %collective-permute-start.1 = (f32[4,32,8,128]{3,2,1,0:T(8,128)S(1)}, f32[4,32,8,128]{3,2,1,0:T(8,128)S(1)}, u32[]{:S(2)}, u32[]{:S(2)}) collective-permute-start(f32[4,32,8,128]{3,2,1,0:T(8,128)S(1)} %get-tuple-element.10), channel_id=1, source_target_pairs={{0,4},{4,8},{8,12},{12,16},{16,20},{20,24},{24,28},{28,32},{32,36}... | collective-permute-start | bytes 1572872 | tf_op jit(solution)/shard_map/ppermute | solution.py:444
  36.2 7.0 %collective-permute-start.3 = (f32[32,8,128]{2,1,0:T(8,128)S(1)}, f32[32,8,128]{2,1,0:T(8,128)S(1)}, u32[]{:S(2)}, u32[]{:S(2)}) collective-permute-start(f32[32,8,128]{2,1,0:T(8,128)S(1)} %get-tuple-element.11.own), channel_id=1, source_target_pairs={{4,0},{8,4},{12,8},{16,12},{20,16},{24,20},{28,24},{32,28},{36,32}... | collective-permute-start | bytes 393224 | tf_op jit(solution)/shard_map/ppermute | solution.py:444
  38.2 6.3 %collective-permute-start.2 = (f32[32,8,128]{2,1,0:T(8,128)S(1)}, f32[32,8,128]{2,1,0:T(8,128)S(1)}, u32[]{:S(2)}, u32[]{:S(2)}) collective-permute-start(f32[32,8,128]{2,1,0:T(8,128)S(1)} %get-tuple-element.11.own), channel_id=1, source_target_pairs={{0,4},{4,8},{8,12},{12,16},{16,20},{20,24},{24,28},{28,32},{32,36}... | collective-permute-start | bytes 393224 | tf_op jit(solution)/shard_map/ppermute | solution.py:444
  45.7 29.5 %all-to-all-start = ((f32[128,2,128]{2,1,0:T(2,128)}), f32[128,2,128]{2,1,0:T(2,128)S(1)}, u32[]{:S(2)}, u32[]{:S(2)}) async-start(f32[128,2,128]{2,1,0:T(2,128)} %bitcast.1), calls=%async_computation | async-start | bytes 262144 | tf_op jit(solution)/shard_map/all_to_all | solution.py:486
  62.4 5.0 %collective-permute-start.4 = (f32[4,4,8,128]{3,2,1,0:T(8,128)S(1)}, f32[4,4,8,128]{3,2,1,0:T(8,128)S(1)}, u32[]{:S(2)}, u32[]{:S(2)}) collective-permute-start(f32[4,4,8,128]{3,2,1,0:T(8,128)S(1)} %get-tuple-element.13), channel_id=1, source_target_pairs={{0,8},{4,12},{8,16},{12,20},{16,24},{20,28},{24,32},{28,36},{32,40... | collective-permute-start | bytes 196616 | tf_op jit(solution)/shard_map/ppermute | solution.py:444
  65.7 5.3 %collective-permute-start.5 = (f32[4,4,8,128]{3,2,1,0:T(8,128)S(1)}, f32[4,4,8,128]{3,2,1,0:T(8,128)S(1)}, u32[]{:S(2)}, u32[]{:S(2)}) collective-permute-start(f32[4,4,8,128]{3,2,1,0:T(8,128)S(1)} %get-tuple-element.14), channel_id=1, source_target_pairs={{8,0},{12,4},{16,8},{20,12},{24,16},{28,20},{32,24},{36,28},{40,32... | collective-permute-start | bytes 196616 | tf_op jit(solution)/shard_map/ppermute | solution.py:444

commit v4 on v3

--- a/solution.py
+++ b/solution.py
@@ -109,18 +109,31 @@
         ref[...] = jnp.zeros(ref.shape, ref.dtype)
 
 
-def spread_kernel(whole, to_right, to_left):
-    for n in range(4):
-        to_right[n, 0:13] = whole[n, 3:16]
-        to_right[n, 13:25] = whole[n, 20:32]
-        to_right[n, 25:32] = whole[n, 33:40]
-        to_left[n, 0:13] = whole[n, 0:13]
-        to_left[n, 13:25] = whole[n, 16:28]
-        to_left[n, 25:32] = whole[n, 32:39]
-
-
-def first_kernel(right, own, left, slab, send, weights0, beside0, weights1, beside1, buf1, sums, sums1, tmp):
+class Chosen:
+    def __init__(self, which, yes, no):
+        self.which, self.yes, self.no = which, yes, no
+
+    def __getitem__(self, at):
+        return jnp.where(self.which, self.yes[at], self.no[at])
+
+
+def sides(abroad, home):
+    even = lax.axis_index("wide") % 2 == 0
+    return Chosen(even, abroad, home), Chosen(even, home, abroad)
+
+
+def spread_kernel(whole, abroad, home):
+    odd = lax.axis_index("wide") % 2
+    for out, right in ((abroad, odd), (home, 1 - odd)):
+        for n in range(4):
+            out[n, 0:13] = whole[n, pl.ds(3 * right, 13)]
+            out[n, 13:25] = whole[n, pl.ds(16 + 4 * right, 12)]
+            out[n, 25:32] = whole[n, pl.ds(32 + right, 7)]
+
+
+def first_kernel(abroad, own, home, slab, send, weights0, beside0, weights1, beside1, buf1, sums, sums1, tmp):
     wide = lax.axis_index("wide")
+    left, right = sides(abroad, home)
     k0, f0, u0 = [(slab.at[2 * a], slab.at[2 * a + 1]) for a in range(3)]
     fine = Level(0, 24, 32, weights0, beside0)
     zeroed(u0[0])
@@ -209,8 +222,9 @@
             slab[2 + c, base + t] = part[28 + 2 * c + t]
 
 
-def second_kernel(left, own, right, out, near_low, near_high, slab, weights, beside):
+def second_kernel(home, own, abroad, out, near_low, near_high, slab, weights, beside):
     wide = lax.axis_index("wide")
+    left, right = sides(abroad, home)
     level = Level(2, 16, 8, weights, beside)
     k, f, u = [(slab.at[2 * a], slab.at[2 * a + 1]) for a in range(3)]
     zeroed(slab)
@@ -330,9 +344,10 @@
     lax.fori_loop(0, iters - 1, advance, advance(0, None))
 
 
-def third_kernel(data, far_left, left, own, right, far_right, slab0, pressure, residual, answer, vectors, faces,
+def third_kernel(data, far_left, home, own, abroad, far_right, slab0, pressure, residual, answer, vectors, faces,
                  weights2, beside2, slab2, weights1, beside1, buf1, grow1, weights0, beside0, u0, grow0):
     wide, narrow = lax.axis_index("wide"), lax.axis_index("narrow")
+    left, right = sides(abroad, home)
     size = lax.axis_size("wide")
     level = Level(2, 16, 8, weights2, beside2)
     k, f, up2 = [(slab2.at[2 * a], slab2.at[2 * a + 1]) for a in range(3)]
@@ -444,19 +459,23 @@
     return lax.ppermute(block, "wide", pairs)
 
 
+def swapped(block, first):
+    starts = range(first, lax.axis_size("wide") - 1, 2)
+    return lax.ppermute(block, "wide", [pair for i in starts for pair in ((i, i + 1), (i + 1, i))])
+
+
 def local(rhs, coefficient, guess):
     shape = (8, 8, LANES)
     odd = (lax.broadcasted_iota(jnp.int32, shape, 1) + lax.broadcasted_iota(jnp.int32, shape, 2)) % 2 == 1
     packed = jnp.where(odd, guess[0::2], guess[1::2])
     whole = lax.all_gather(jnp.concatenate([coefficient, rhs, packed], axis=0), "narrow")
-    to_right, to_left = pl.pallas_call(
+    for_abroad, for_home = pl.pallas_call(
         spread_kernel,
         out_shape=(f32(4, 32, 8, LANES), f32(4, 32, 8, LANES)),
         compiler_params=PARAMS,
         name="spread",
     )(whole)
-    right = shifted(to_left, -1)
-    left = shifted(to_right, 1)
+    abroad, home = swapped(for_abroad, 1), swapped(for_home, 0)
     slab0, send = pl.pallas_call(
         first_kernel,
         out_shape=(f32(6, 24, 32, LANES), f32(32, 8, LANES)),
@@ -472,8 +491,8 @@
         ],
         compiler_params=PARAMS,
         name="first",
-    )(right, whole, left)
-    near = (shifted(send, 1), send, shifted(send, -1))
+    )(abroad, whole, home)
+    near = (swapped(send, 0), send, swapped(send, 1))
     count = lax.axis_size("wide")
     out3, near_low, near_high = pl.pallas_call(
         second_kernel,

time: 84 us -> 80.2 us (0.955)
  waiting for transfers between devices: 16.2 us -> 11.7 us
    ppermute x6 -> x2, starting transfers between devices: 23.3 us -> 4.58 us  [shifted(): return lax.ppermute(block, 'wide', pairs)]
    ppermute x0 -> x4, starting transfers between devices: none -> 16.8 us  [swapped(): lax.ppermute(block, 'wide', [pair for i in starts for pair in ((i, i + 1)...]
    ppermute x6 -> x2, waiting for transfers between devices: 12 us -> 4 us  [shifted(): return lax.ppermute(block, 'wide', pairs)]
    ppermute x0 -> x4, waiting for transfers between devices: none -> 3.62 us  [swapped(): lax.ppermute(block, 'wide', [pair for i in starts for pair in ((i, i + 1)...]
    all_to_all x1, starting transfers between devices: 16.8 us -> 19.3 us  [local(): lax.all_to_all(out3.reshape(count, 2, LANES), 'wide', 0, 0)]
  transfers between devices with their start and end apart: 7 -> 7, of which waited for: 7 -> 6; matrix products, arithmetic and copies ran while one was open for 0% -> 0% of each run, Pallas kernels for 0% -> 0%
where the time goes in v4:
time: 80.2 us; the launch traced here: 79.8 us
  starting transfers between devices  40.6 us (51%)
  Pallas kernels  13.8 us (17%)
  waiting for transfers between devices  11.7 us (15%)
  blocking collectives  11.3 us (14%)
  other arithmetic  1.67 us (2%)
    all_to_all x1, starting transfers between devices, local(): lax.all_to_all(out3.reshape(count, 2, LANES), 'wide', 0, 0)  19.3 us
    ppermute x4, starting transfers between devices, swapped(): lax.ppermute(block, 'wide', [pair for i in starts for pair in ((i, i + 1)...  16.8 us
    all_gather x1, blocking collectives, local(): lax.all_gather(jnp.concatenate([coefficient, rhs, packed], axis=0), 'narr...  11.3 us
    pallas_call x1, Pallas kernels, local(): pl.pallas_call(third_kernel, out_shape=(f32(16, 8, LANES), f32(16, 8, LAN...  8.47 us
    ppermute x2, starting transfers between devices, shifted(): return lax.ppermute(block, 'wide', pairs)  4.58 us
    all_to_all x1, waiting for transfers between devices, local(): lax.all_to_all(out3.reshape(count, 2, LANES), 'wide', 0, 0)  4.12 us
    pallas_call x1, Pallas kernels, local(): pl.pallas_call(first_kernel, out_shape=(f32(6, 24, 32, LANES), f32(32, 8,...  4.03 us
    ppermute x2, waiting for transfers between devices, shifted(): return lax.ppermute(block, 'wide', pairs)  4 us
  transfers between devices with their start and end apart: 7, of which 6 were waited for; matrix products, arithmetic and copies ran while one was open for 0% of the time, Pallas kernels for 0%

profile of v4, /device:TPU:1, one launch (start us, length us, event | category | flops | bytes accessed | tf_op | source)
XLA Modules:
  0.0 79.8 jit_solution(5459779937647951788)
XLA Ops:
  0.6 0.8 slice_select_fusion
  1.4 0.9 %pad_maximum_fusion = f32[40,8,128]{2,1,0:T(8,128)S(1)} fusion(f32[8,8,128]{2,1,0:T(8,128)S(1)} %slice_select_fusion, f32[16,8,128]{2,1,0:T(8,128)} %param.3, f32[16,8,128]{2,1,0:T(8,128)} %param.4), kind=kLoop, calls=%fused_computation | loop fusion | flops 81920 | bytes 327680 | tf_op jit(solution)/shard_map/concatenate | solution.py:471
  2.3 11.3 %all-gather = f32[160,8,128]{2,1,0:T(8,128)S(1)} all-gather(f32[40,8,128]{2,1,0:T(8,128)S(1)} %pad_maximum_fusion), channel_id=2, replica_groups=mesh['wide'=128,'narrow'=4] {'narrow'}, dimensions={0}, use_global_device_ids=true | all-gather | bytes 819200 | tf_op jit(solution)/shard_map/all_gather | solution.py:471
  13.6 0.1 spread.1
  13.7 6.7 %collective-permute-start = (f32[4,32,8,128]{3,2,1,0:T(8,128)S(1)}, f32[4,32,8,128]{3,2,1,0:T(8,128)S(1)}, u32[]{:S(2)}, u32[]{:S(2)}) collective-permute-start(f32[4,32,8,128]{3,2,1,0:T(8,128)S(1)} %get-tuple-element.9), channel_id=1, source_target_pairs={{4,8},{8,4},{12,16},{16,12},{20,24},{24,20},{28,32},{32,28},{36,40... | collective-permute-start | bytes 1572872 | tf_op jit(solution)/shard_map/ppermute | solution.py:464
  20.4 4.5 %collective-permute-start.1 = (f32[4,32,8,128]{3,2,1,0:T(8,128)S(1)}, f32[4,32,8,128]{3,2,1,0:T(8,128)S(1)}, u32[]{:S(2)}, u32[]{:S(2)}) collective-permute-start(f32[4,32,8,128]{3,2,1,0:T(8,128)S(1)} %get-tuple-element.10), channel_id=1, source_target_pairs={{0,4},{4,0},{8,12},{12,8},{16,20},{20,16},{24,28},{28,24},{32,36},... | collective-permute-start | bytes 1572872 | tf_op jit(solution)/shard_map/ppermute | solution.py:464
  24.9 2.3 %collective-permute-done.abroad = f32[4,32,8,128]{3,2,1,0:T(8,128)S(1)} collective-permute-done((f32[4,32,8,128]{3,2,1,0:T(8,128)S(1)}, f32[4,32,8,128]{3,2,1,0:T(8,128)S(1)}, u32[]{:S(2)}, u32[]{:S(2)}) %collective-permute-start) | collective-permute-done | bytes 524320 | tf_op jit(solution)/shard_map/ppermute | solution.py:464
  27.2 0.0 collective-permute-done.1.home
  27.2 4.0 %first.1 = (f32[6,24,32,128]{3,2,1,0:T(8,128)S(1)}, f32[32,8,128]{2,1,0:T(8,128)S(1)}) custom-call(f32[4,32,8,128]{3,2,1,0:T(8,128)S(1)} %collective-permute-done.abroad, f32[4,40,8,128]{3,2,1,0:T(8,128)S(1)} %bitcast.4, f32[4,32,8,128]{3,2,1,0:T(8,128)S(1)} %collective-permute-done.1.home), custom_call_target="tpu_custom_call" | custom-call | tf_op jit(solution)/shard_map/first/pallas_call | solution.py:479
  31.3 3.6 %collective-permute-start.3 = (f32[32,8,128]{2,1,0:T(8,128)S(1)}, f32[32,8,128]{2,1,0:T(8,128)S(1)}, u32[]{:S(2)}, u32[]{:S(2)}) collective-permute-start(f32[32,8,128]{2,1,0:T(8,128)S(1)} %get-tuple-element.11.own), channel_id=1, source_target_pairs={{4,8},{8,4},{12,16},{16,12},{20,24},{24,20},{28,32},{32,28},{36,40... | collective-permute-start | bytes 393224 | tf_op jit(solution)/shard_map/ppermute | solution.py:464
  34.9 1.9 %collective-permute-start.2 = (f32[32,8,128]{2,1,0:T(8,128)S(1)}, f32[32,8,128]{2,1,0:T(8,128)S(1)}, u32[]{:S(2)}, u32[]{:S(2)}) collective-permute-start(f32[32,8,128]{2,1,0:T(8,128)S(1)} %get-tuple-element.11.own), channel_id=1, source_target_pairs={{0,4},{4,0},{8,12},{12,8},{16,20},{20,16},{24,28},{28,24},{32,36},... | collective-permute-start | bytes 393224 | tf_op jit(solution)/shard_map/ppermute | solution.py:464
  36.8 0.7 collective-permute-done.3.abroad
  37.5 0.6 collective-permute-done.2.home
  38.2 1.2 %second.1 = (f32[256,128]{1,0:T(8,128)}, f32[4,4,8,128]{3,2,1,0:T(8,128)S(1)}, f32[4,4,8,128]{3,2,1,0:T(8,128)S(1)}) custom-call(f32[32,8,128]{2,1,0:T(8,128)S(1)} %collective-permute-done.2.home, f32[32,8,128]{2,1,0:T(8,128)S(1)} %get-tuple-element.11.own, f32[32,8,128]{2,1,0:T(8,128)S(1)} %collective-permute-done.3.abroad), custom_call_target="tpu_custom_call" | custom-call | tf_op jit(solution)/shard_map/second/pallas_call | solution.py:497
  39.3 19.3 %all-to-all-start = ((f32[128,2,128]{2,1,0:T(2,128)}), f32[128,2,128]{2,1,0:T(2,128)S(1)}, u32[]{:S(2)}, u32[]{:S(2)}) async-start(f32[128,2,128]{2,1,0:T(2,128)} %bitcast.1), calls=%async_computation | async-start | bytes 262144 | tf_op jit(solution)/shard_map/all_to_all | solution.py:505
  58.6 3.3 %collective-permute-start.4 = (f32[4,4,8,128]{3,2,1,0:T(8,128)S(1)}, f32[4,4,8,128]{3,2,1,0:T(8,128)S(1)}, u32[]{:S(2)}, u32[]{:S(2)}) collective-permute-start(f32[4,4,8,128]{3,2,1,0:T(8,128)S(1)} %get-tuple-element.13), channel_id=1, source_target_pairs={{0,8},{4,12},{8,16},{12,20},{16,24},{20,28},{24,32},{28,36},{32,40... | collective-permute-start | bytes 196616 | tf_op jit(solution)/shard_map/ppermute | solution.py:459
  61.9 1.3 %collective-permute-start.5 = (f32[4,4,8,128]{3,2,1,0:T(8,128)S(1)}, f32[4,4,8,128]{3,2,1,0:T(8,128)S(1)}, u32[]{:S(2)}, u32[]{:S(2)}) collective-permute-start(f32[4,4,8,128]{3,2,1,0:T(8,128)S(1)} %get-tuple-element.14), channel_id=1, source_target_pairs={{8,0},{12,4},{16,8},{20,12},{24,16},{28,20},{32,24},{36,28},{40,32... | collective-permute-start | bytes 196616 | tf_op jit(solution)/shard_map/ppermute | solution.py:459
  63.2 0.4 collective-permute-done.4.far_left
  63.6 3.6 %collective-permute-done.5.far_right = f32[4,4,8,128]{3,2,1,0:T(8,128)S(1)} collective-permute-done((f32[4,4,8,128]{3,2,1,0:T(8,128)S(1)}, f32[4,4,8,128]{3,2,1,0:T(8,128)S(1)}, u32[]{:S(2)}, u32[]{:S(2)}) %collective-permute-start.5) | collective-permute-done | bytes 65568 | tf_op jit(solution)/shard_map/ppermute | solution.py:459
  67.2 4.1 %all-to-all-done = f32[128,2,128]{2,1,0:T(2,128)S(1)} async-done(((f32[128,2,128]{2,1,0:T(2,128)}), f32[128,2,128]{2,1,0:T(2,128)S(1)}, u32[]{:S(2)}, u32[]{:S(2)}) %all-to-all-start) | async-done | bytes 131104 | tf_op jit(solution)/shard_map/all_to_all | solution.py:505
  71.4 8.5 %third.1 = (f32[16,8,128]{2,1,0:T(8,128)}, f32[16,8,128]{2,1,0:T(8,128)}) custom-call(f32[256,128]{1,0:T(8,128)S(1)} %bitcast.5, f32[4,4,8,128]{3,2,1,0:T(8,128)S(1)} %collective-permute-done.4.far_left, f32[32,8,128]{2,1,0:T(8,128)S(1)} %collective-permute-done.2.home, f32[32,8,128]{2,1,0:T(8,128)S(1)} %get-tuple-element.11.own, ...), custom_call_target="tpu_custom_call" | custom-call | tf_op jit(solution)/shard_map/third/pallas_call | solution.py:506
Async XLA Ops:
  13.7 13.5 %collective-permute-start = (f32[4,32,8,128]{3,2,1,0:T(8,128)S(1)}, f32[4,32,8,128]{3,2,1,0:T(8,128)S(1)}, u32[]{:S(2)}, u32[]{:S(2)}) collective-permute-start(f32[4,32,8,128]{3,2,1,0:T(8,128)S(1)} %get-tuple-element.9), channel_id=1, source_target_pairs={{4,8},{8,4},{12,16},{16,12},{20,24},{24,20},{28,32},{32,28},{36,40... | collective-permute-start | bytes 1572872 | tf_op jit(solution)/shard_map/ppermute | solution.py:464
  20.4 6.9 %collective-permute-start.1 = (f32[4,32,8,128]{3,2,1,0:T(8,128)S(1)}, f32[4,32,8,128]{3,2,1,0:T(8,128)S(1)}, u32[]{:S(2)}, u32[]{:S(2)}) collective-permute-start(f32[4,32,8,128]{3,2,1,0:T(8,128)S(1)} %get-tuple-element.10), channel_id=1, source_target_pairs={{0,4},{4,0},{8,12},{12,8},{16,20},{20,16},{24,28},{28,24},{32,36},... | collective-permute-start | bytes 1572872 | tf_op jit(solution)/shard_map/ppermute | solution.py:464
  31.3 6.3 %collective-permute-start.3 = (f32[32,8,128]{2,1,0:T(8,128)S(1)}, f32[32,8,128]{2,1,0:T(8,128)S(1)}, u32[]{:S(2)}, u32[]{:S(2)}) collective-permute-start(f32[32,8,128]{2,1,0:T(8,128)S(1)} %get-tuple-element.11.own), channel_id=1, source_target_pairs={{4,8},{8,4},{12,16},{16,12},{20,24},{24,20},{28,32},{32,28},{36,40... | collective-permute-start | bytes 393224 | tf_op jit(solution)/shard_map/ppermute | solution.py:464
  34.9 3.2 %collective-permute-start.2 = (f32[32,8,128]{2,1,0:T(8,128)S(1)}, f32[32,8,128]{2,1,0:T(8,128)S(1)}, u32[]{:S(2)}, u32[]{:S(2)}) collective-permute-start(f32[32,8,128]{2,1,0:T(8,128)S(1)} %get-tuple-element.11.own), channel_id=1, source_target_pairs={{0,4},{4,0},{8,12},{12,8},{16,20},{20,16},{24,28},{28,24},{32,36},... | collective-permute-start | bytes 393224 | tf_op jit(solution)/shard_map/ppermute | solution.py:464
  39.3 32.0 %all-to-all-start = ((f32[128,2,128]{2,1,0:T(2,128)}), f32[128,2,128]{2,1,0:T(2,128)S(1)}, u32[]{:S(2)}, u32[]{:S(2)}) async-start(f32[128,2,128]{2,1,0:T(2,128)} %bitcast.1), calls=%async_computation | async-start | bytes 262144 | tf_op jit(solution)/shard_map/all_to_all | solution.py:505
  58.6 5.0 %collective-permute-start.4 = (f32[4,4,8,128]{3,2,1,0:T(8,128)S(1)}, f32[4,4,8,128]{3,2,1,0:T(8,128)S(1)}, u32[]{:S(2)}, u32[]{:S(2)}) collective-permute-start(f32[4,4,8,128]{3,2,1,0:T(8,128)S(1)} %get-tuple-element.13), channel_id=1, source_target_pairs={{0,8},{4,12},{8,16},{12,20},{16,24},{20,28},{24,32},{28,36},{32,40... | collective-permute-start | bytes 196616 | tf_op jit(solution)/shard_map/ppermute | solution.py:459
  61.9 5.3 %collective-permute-start.5 = (f32[4,4,8,128]{3,2,1,0:T(8,128)S(1)}, f32[4,4,8,128]{3,2,1,0:T(8,128)S(1)}, u32[]{:S(2)}, u32[]{:S(2)}) collective-permute-start(f32[4,4,8,128]{3,2,1,0:T(8,128)S(1)} %get-tuple-element.14), channel_id=1, source_target_pairs={{8,0},{12,4},{16,8},{20,12},{24,16},{28,20},{32,24},{36,28},{40,32... | collective-permute-start | bytes 196616 | tf_op jit(solution)/shard_map/ppermute | solution.py:459

commit v5 on v4

--- a/solution.py
+++ b/solution.py
@@ -341,7 +341,9 @@
 
     for v, value in enumerate(source):
         remain[v] = value
-    lax.fori_loop(0, iters - 1, advance, advance(0, None))
+    carry = None
+    for step in range(iters):
+        carry = advance(step, carry)
 
 
 def third_kernel(data, far_left, home, own, abroad, far_right, slab0, pressure, residual, answer, vectors, faces,

time: 80.2 us -> 79.9 us (level)
  no operation moved by 1% of the time
where the time goes in v5:
time: 79.9 us; the launch traced here: 79.5 us
  starting transfers between devices  40.6 us (51%)
  Pallas kernels  13.4 us (17%)
  waiting for transfers between devices  11.7 us (15%)
  blocking collectives  11.3 us (14%)
  other arithmetic  1.67 us (2%)
    all_to_all x1, starting transfers between devices, local(): lax.all_to_all(out3.reshape(count, 2, LANES), 'wide', 0, 0)  19.3 us
    ppermute x4, starting transfers between devices, swapped(): lax.ppermute(block, 'wide', [pair for i in starts for pair in ((i, i + 1)...  16.8 us
    all_gather x1, blocking collectives, local(): lax.all_gather(jnp.concatenate([coefficient, rhs, packed], axis=0), 'narr...  11.3 us
    pallas_call x1, Pallas kernels, local(): pl.pallas_call(third_kernel, out_shape=(f32(16, 8, LANES), f32(16, 8, LAN...  8.13 us
    ppermute x2, starting transfers between devices, shifted(): return lax.ppermute(block, 'wide', pairs)  4.58 us
    all_to_all x1, waiting for transfers between devices, local(): lax.all_to_all(out3.reshape(count, 2, LANES), 'wide', 0, 0)  4.12 us
    pallas_call x1, Pallas kernels, local(): pl.pallas_call(first_kernel, out_shape=(f32(6, 24, 32, LANES), f32(32, 8,...  4.03 us
    ppermute x2, waiting for transfers between devices, shifted(): return lax.ppermute(block, 'wide', pairs)  4 us
  transfers between devices with their start and end apart: 7, of which 6 were waited for; matrix products, arithmetic and copies ran while one was open for 0% of the time, Pallas kernels for 0%

profile of v5, /device:TPU:1, one launch (start us, length us, event | category | flops | bytes accessed | tf_op | source)
XLA Modules:
  0.0 79.5 jit_solution(2055380469761047547)
XLA Ops:
  0.6 0.8 slice_select_fusion
  1.4 0.9 %pad_maximum_fusion = f32[40,8,128]{2,1,0:T(8,128)S(1)} fusion(f32[8,8,128]{2,1,0:T(8,128)S(1)} %slice_select_fusion, f32[16,8,128]{2,1,0:T(8,128)} %param.3, f32[16,8,128]{2,1,0:T(8,128)} %param.4), kind=kLoop, calls=%fused_computation | loop fusion | flops 81920 | bytes 327680 | tf_op jit(solution)/shard_map/concatenate | solution.py:473
  2.3 11.3 %all-gather = f32[160,8,128]{2,1,0:T(8,128)S(1)} all-gather(f32[40,8,128]{2,1,0:T(8,128)S(1)} %pad_maximum_fusion), channel_id=2, replica_groups=mesh['wide'=128,'narrow'=4] {'narrow'}, dimensions={0}, use_global_device_ids=true | all-gather | bytes 819200 | tf_op jit(solution)/shard_map/all_gather | solution.py:473
  13.6 0.1 spread.1
  13.7 6.7 %collective-permute-start = (f32[4,32,8,128]{3,2,1,0:T(8,128)S(1)}, f32[4,32,8,128]{3,2,1,0:T(8,128)S(1)}, u32[]{:S(2)}, u32[]{:S(2)}) collective-permute-start(f32[4,32,8,128]{3,2,1,0:T(8,128)S(1)} %get-tuple-element.9), channel_id=1, source_target_pairs={{4,8},{8,4},{12,16},{16,12},{20,24},{24,20},{28,32},{32,28},{36,40... | collective-permute-start | bytes 1572872 | tf_op jit(solution)/shard_map/ppermute | solution.py:466
  20.4 4.5 %collective-permute-start.1 = (f32[4,32,8,128]{3,2,1,0:T(8,128)S(1)}, f32[4,32,8,128]{3,2,1,0:T(8,128)S(1)}, u32[]{:S(2)}, u32[]{:S(2)}) collective-permute-start(f32[4,32,8,128]{3,2,1,0:T(8,128)S(1)} %get-tuple-element.10), channel_id=1, source_target_pairs={{0,4},{4,0},{8,12},{12,8},{16,20},{20,16},{24,28},{28,24},{32,36},... | collective-permute-start | bytes 1572872 | tf_op jit(solution)/shard_map/ppermute | solution.py:466
  24.9 2.3 %collective-permute-done.abroad = f32[4,32,8,128]{3,2,1,0:T(8,128)S(1)} collective-permute-done((f32[4,32,8,128]{3,2,1,0:T(8,128)S(1)}, f32[4,32,8,128]{3,2,1,0:T(8,128)S(1)}, u32[]{:S(2)}, u32[]{:S(2)}) %collective-permute-start) | collective-permute-done | bytes 524320 | tf_op jit(solution)/shard_map/ppermute | solution.py:466
  27.2 0.0 collective-permute-done.1.home
  27.2 4.0 %first.1 = (f32[6,24,32,128]{3,2,1,0:T(8,128)S(1)}, f32[32,8,128]{2,1,0:T(8,128)S(1)}) custom-call(f32[4,32,8,128]{3,2,1,0:T(8,128)S(1)} %collective-permute-done.abroad, f32[4,40,8,128]{3,2,1,0:T(8,128)S(1)} %bitcast.4, f32[4,32,8,128]{3,2,1,0:T(8,128)S(1)} %collective-permute-done.1.home), custom_call_target="tpu_custom_call" | custom-call | tf_op jit(solution)/shard_map/first/pallas_call | solution.py:481
  31.3 3.6 %collective-permute-start.3 = (f32[32,8,128]{2,1,0:T(8,128)S(1)}, f32[32,8,128]{2,1,0:T(8,128)S(1)}, u32[]{:S(2)}, u32[]{:S(2)}) collective-permute-start(f32[32,8,128]{2,1,0:T(8,128)S(1)} %get-tuple-element.11.own), channel_id=1, source_target_pairs={{4,8},{8,4},{12,16},{16,12},{20,24},{24,20},{28,32},{32,28},{36,40... | collective-permute-start | bytes 393224 | tf_op jit(solution)/shard_map/ppermute | solution.py:466
  34.9 1.9 %collective-permute-start.2 = (f32[32,8,128]{2,1,0:T(8,128)S(1)}, f32[32,8,128]{2,1,0:T(8,128)S(1)}, u32[]{:S(2)}, u32[]{:S(2)}) collective-permute-start(f32[32,8,128]{2,1,0:T(8,128)S(1)} %get-tuple-element.11.own), channel_id=1, source_target_pairs={{0,4},{4,0},{8,12},{12,8},{16,20},{20,16},{24,28},{28,24},{32,36},... | collective-permute-start | bytes 393224 | tf_op jit(solution)/shard_map/ppermute | solution.py:466
  36.8 0.7 collective-permute-done.3.abroad
  37.5 0.6 collective-permute-done.2.home
  38.2 1.2 %second.1 = (f32[256,128]{1,0:T(8,128)}, f32[4,4,8,128]{3,2,1,0:T(8,128)S(1)}, f32[4,4,8,128]{3,2,1,0:T(8,128)S(1)}) custom-call(f32[32,8,128]{2,1,0:T(8,128)S(1)} %collective-permute-done.2.home, f32[32,8,128]{2,1,0:T(8,128)S(1)} %get-tuple-element.11.own, f32[32,8,128]{2,1,0:T(8,128)S(1)} %collective-permute-done.3.abroad), custom_call_target="tpu_custom_call" | custom-call | tf_op jit(solution)/shard_map/second/pallas_call | solution.py:499
  39.3 19.3 %all-to-all-start = ((f32[128,2,128]{2,1,0:T(2,128)}), f32[128,2,128]{2,1,0:T(2,128)S(1)}, u32[]{:S(2)}, u32[]{:S(2)}) async-start(f32[128,2,128]{2,1,0:T(2,128)} %bitcast.1), calls=%async_computation | async-start | bytes 262144 | tf_op jit(solution)/shard_map/all_to_all | solution.py:507
  58.6 3.3 %collective-permute-start.4 = (f32[4,4,8,128]{3,2,1,0:T(8,128)S(1)}, f32[4,4,8,128]{3,2,1,0:T(8,128)S(1)}, u32[]{:S(2)}, u32[]{:S(2)}) collective-permute-start(f32[4,4,8,128]{3,2,1,0:T(8,128)S(1)} %get-tuple-element.13), channel_id=1, source_target_pairs={{0,8},{4,12},{8,16},{12,20},{16,24},{20,28},{24,32},{28,36},{32,40... | collective-permute-start | bytes 196616 | tf_op jit(solution)/shard_map/ppermute | solution.py:461
  61.9 1.3 %collective-permute-start.5 = (f32[4,4,8,128]{3,2,1,0:T(8,128)S(1)}, f32[4,4,8,128]{3,2,1,0:T(8,128)S(1)}, u32[]{:S(2)}, u32[]{:S(2)}) collective-permute-start(f32[4,4,8,128]{3,2,1,0:T(8,128)S(1)} %get-tuple-element.14), channel_id=1, source_target_pairs={{8,0},{12,4},{16,8},{20,12},{24,16},{28,20},{32,24},{36,28},{40,32... | collective-permute-start | bytes 196616 | tf_op jit(solution)/shard_map/ppermute | solution.py:461
  63.2 0.4 collective-permute-done.4.far_left
  63.6 3.6 %collective-permute-done.5.far_right = f32[4,4,8,128]{3,2,1,0:T(8,128)S(1)} collective-permute-done((f32[4,4,8,128]{3,2,1,0:T(8,128)S(1)}, f32[4,4,8,128]{3,2,1,0:T(8,128)S(1)}, u32[]{:S(2)}, u32[]{:S(2)}) %collective-permute-start.5) | collective-permute-done | bytes 65568 | tf_op jit(solution)/shard_map/ppermute | solution.py:461
  67.2 4.1 %all-to-all-done = f32[128,2,128]{2,1,0:T(2,128)S(1)} async-done(((f32[128,2,128]{2,1,0:T(2,128)}), f32[128,2,128]{2,1,0:T(2,128)S(1)}, u32[]{:S(2)}, u32[]{:S(2)}) %all-to-all-start) | async-done | bytes 131104 | tf_op jit(solution)/shard_map/all_to_all | solution.py:507
  71.4 8.1 %third.1 = (f32[16,8,128]{2,1,0:T(8,128)}, f32[16,8,128]{2,1,0:T(8,128)}) custom-call(f32[256,128]{1,0:T(8,128)S(1)} %bitcast.5, f32[4,4,8,128]{3,2,1,0:T(8,128)S(1)} %collective-permute-done.4.far_left, f32[32,8,128]{2,1,0:T(8,128)S(1)} %collective-permute-done.2.home, f32[32,8,128]{2,1,0:T(8,128)S(1)} %get-tuple-element.11.own, ...), custom_call_target="tpu_custom_call" | custom-call | tf_op jit(solution)/shard_map/third/pallas_call | solution.py:508
Async XLA Ops:
  13.7 13.5 %collective-permute-start = (f32[4,32,8,128]{3,2,1,0:T(8,128)S(1)}, f32[4,32,8,128]{3,2,1,0:T(8,128)S(1)}, u32[]{:S(2)}, u32[]{:S(2)}) collective-permute-start(f32[4,32,8,128]{3,2,1,0:T(8,128)S(1)} %get-tuple-element.9), channel_id=1, source_target_pairs={{4,8},{8,4},{12,16},{16,12},{20,24},{24,20},{28,32},{32,28},{36,40... | collective-permute-start | bytes 1572872 | tf_op jit(solution)/shard_map/ppermute | solution.py:466
  20.4 6.9 %collective-permute-start.1 = (f32[4,32,8,128]{3,2,1,0:T(8,128)S(1)}, f32[4,32,8,128]{3,2,1,0:T(8,128)S(1)}, u32[]{:S(2)}, u32[]{:S(2)}) collective-permute-start(f32[4,32,8,128]{3,2,1,0:T(8,128)S(1)} %get-tuple-element.10), channel_id=1, source_target_pairs={{0,4},{4,0},{8,12},{12,8},{16,20},{20,16},{24,28},{28,24},{32,36},... | collective-permute-start | bytes 1572872 | tf_op jit(solution)/shard_map/ppermute | solution.py:466
  31.3 6.3 %collective-permute-start.3 = (f32[32,8,128]{2,1,0:T(8,128)S(1)}, f32[32,8,128]{2,1,0:T(8,128)S(1)}, u32[]{:S(2)}, u32[]{:S(2)}) collective-permute-start(f32[32,8,128]{2,1,0:T(8,128)S(1)} %get-tuple-element.11.own), channel_id=1, source_target_pairs={{4,8},{8,4},{12,16},{16,12},{20,24},{24,20},{28,32},{32,28},{36,40... | collective-permute-start | bytes 393224 | tf_op jit(solution)/shard_map/ppermute | solution.py:466
  34.9 3.2 %collective-permute-start.2 = (f32[32,8,128]{2,1,0:T(8,128)S(1)}, f32[32,8,128]{2,1,0:T(8,128)S(1)}, u32[]{:S(2)}, u32[]{:S(2)}) collective-permute-start(f32[32,8,128]{2,1,0:T(8,128)S(1)} %get-tuple-element.11.own), channel_id=1, source_target_pairs={{0,4},{4,0},{8,12},{12,8},{16,20},{20,16},{24,28},{28,24},{32,36},... | collective-permute-start | bytes 393224 | tf_op jit(solution)/shard_map/ppermute | solution.py:466
  39.3 32.0 %all-to-all-start = ((f32[128,2,128]{2,1,0:T(2,128)}), f32[128,2,128]{2,1,0:T(2,128)S(1)}, u32[]{:S(2)}, u32[]{:S(2)}) async-start(f32[128,2,128]{2,1,0:T(2,128)} %bitcast.1), calls=%async_computation | async-start | bytes 262144 | tf_op jit(solution)/shard_map/all_to_all | solution.py:507
  58.6 5.0 %collective-permute-start.4 = (f32[4,4,8,128]{3,2,1,0:T(8,128)S(1)}, f32[4,4,8,128]{3,2,1,0:T(8,128)S(1)}, u32[]{:S(2)}, u32[]{:S(2)}) collective-permute-start(f32[4,4,8,128]{3,2,1,0:T(8,128)S(1)} %get-tuple-element.13), channel_id=1, source_target_pairs={{0,8},{4,12},{8,16},{12,20},{16,24},{20,28},{24,32},{28,36},{32,40... | collective-permute-start | bytes 196616 | tf_op jit(solution)/shard_map/ppermute | solution.py:461
  61.9 5.3 %collective-permute-start.5 = (f32[4,4,8,128]{3,2,1,0:T(8,128)S(1)}, f32[4,4,8,128]{3,2,1,0:T(8,128)S(1)}, u32[]{:S(2)}, u32[]{:S(2)}) collective-permute-start(f32[4,4,8,128]{3,2,1,0:T(8,128)S(1)} %get-tuple-element.14), channel_id=1, source_target_pairs={{8,0},{12,4},{16,8},{20,12},{24,16},{28,20},{32,24},{36,28},{40,32... | collective-permute-start | bytes 196616 | tf_op jit(solution)/shard_map/ppermute | solution.py:461
